TPU v7x, 32 devices: a whole 2x2x4 slice. The times are simulated.
32 devices in a mesh: fsdp: 16 (over z, y, x), sp: 2 (over core).
Axes of the slice: x: 2, y: 2, z: 4, core: 2. Of those that a mesh axis runs over, the one named last changes fastest.
Arguments:
- latents: bfloat16 [16, 48, 3072], P('fsdp', 'sp'), may hold values from -6 to 6
- step_noise: bfloat16 [16, 48, 3072], P('fsdp', 'sp'), may hold values from -6 to 6
- base_qkv: bfloat16 [3, 3072, 3072], P(None, 'fsdp', 'sp'), may hold values from -1 to 1
- down_qkv: bfloat16 [3, 3072, 64], P(None, 'fsdp'), may hold values from -0.109375 to 0.109375
- up_query_key_value: bfloat16 [3, 64, 3072], P(None, None, 'sp'), may hold values from -0.625 to 0.625
- base_out: bfloat16 [3072, 3072], P('sp', 'fsdp'), may hold values from -0.109375 to 0.109375
- down_out: bfloat16 [3072, 64], P('sp'), may hold values from -0.109375 to 0.109375
- up_out: bfloat16 [64, 3072], P(None, 'fsdp'), may hold values from -0.625 to 0.625
- modulation: float32 [16, 3, 3072], replicated, may hold values from -3 to 3
- timestep: int32 [16], P('fsdp'), may hold values from 0 to 14
Outputs:
- velocity: bfloat16 [16, 48, 3072], P('fsdp', 'sp')
- next_latents: bfloat16 [16, 48, 3072], P('fsdp', 'sp')
Inputs may be any that keep to these rules, and one draw needn't show every extreme that they name: timestep[n] + 1 is also a step of the plan.
All inputs are finite; a program needn't handle non-finite values.
Results may differ from a plain program's by a relative error of at most 0.02.
Values may be sent and summed in bfloat16 or wider, within the bound.
A program may use at most 128 MiB of HBM per device.

v0:
```python
import jax
import jax.numpy as jnp
from jax import lax
from jax.sharding import PartitionSpec as P

HEAD_DIM = 128
NSTEP = 16


EPSILON = 1e-06
SHIFT_FACTOR = 5.0
NOISE_LEVEL = 0.7


def plan_sigma(position):
    ramp = 1.0 - position / NSTEP
    return SHIFT_FACTOR * ramp / (1.0 + (SHIFT_FACTOR - 1.0) * ramp)


def per_device(
    latents,
    step_noise,
    base_qkv,
    down_qkv,
    up_query_key_value,
    base_out,
    down_out,
    up_out,
    modulation,
    timestep,
):
    step_index = timestep[0]
    mod_rows = lax.dynamic_index_in_dim(modulation, step_index, 0, keepdims=False)
    latent_f = latents[0].astype(jnp.float32)
    mean_square = jnp.mean(latent_f * latent_f, axis=-1, keepdims=True)
    normalized_rows = (
        latent_f * lax.rsqrt(mean_square + EPSILON) * (1.0 + mod_rows[1]) + mod_rows[0]
    ).astype(jnp.bfloat16)
    head_cols = base_qkv.shape[2]
    seq_len = normalized_rows.shape[0] * lax.axis_size("sp")
    every_token = lax.all_gather(normalized_rows, "sp", axis=0, tiled=True)
    lowrank = jnp.einsum(
        "prk,pkc->prc", down_qkv, up_query_key_value, preferred_element_type=jnp.float32
    )
    merged_qkv = (base_qkv.astype(jnp.float32) + lowrank).astype(jnp.bfloat16)
    projected = jnp.einsum(
        "lr,prc->plc",
        every_token,
        lax.all_gather(merged_qkv, "fsdp", axis=1, tiled=True),
        preferred_element_type=jnp.float32,
    ).astype(jnp.bfloat16)
    heads_here = head_cols // HEAD_DIM
    split_heads = projected.reshape(3, seq_len, heads_here, HEAD_DIM).transpose(2, 0, 1, 3)

    def one_head(triple):
        scores = jnp.dot(triple[0], triple[1].T, preferred_element_type=jnp.float32) * (
            1.0 / HEAD_DIM**0.5
        )
        attention_weights = jax.nn.softmax(scores, axis=-1).astype(jnp.bfloat16)
        return jnp.dot(attention_weights, triple[2], preferred_element_type=jnp.float32).astype(
            jnp.bfloat16
        )

    per_head = lax.map(one_head, split_heads)
    attention_result = per_head.transpose(1, 0, 2).reshape(seq_len, head_cols)
    merged_out = (
        base_out.astype(jnp.float32) + jnp.dot(down_out, up_out, preferred_element_type=jnp.float32)
    ).astype(jnp.bfloat16)
    full_out = lax.all_gather(merged_out, "fsdp", axis=1, tiled=True)
    block_out = lax.psum_scatter(
        jnp.dot(attention_result, full_out, preferred_element_type=jnp.float32).astype(
            jnp.bfloat16
        ),
        "sp",
        scatter_dimension=0,
        tiled=True,
    ).astype(jnp.float32)
    velocity = ((1.0 + mod_rows[2]) * block_out).astype(jnp.bfloat16)
    position = step_index.astype(jnp.float32)
    step_size = plan_sigma(position + 1.0) - plan_sigma(position)
    next_rows = (
        latent_f
        + step_size * velocity.astype(jnp.float32)
        + NOISE_LEVEL * jnp.sqrt(-step_size) * step_noise[0].astype(jnp.float32)
    )
    return (velocity[None], next_rows.astype(jnp.bfloat16)[None])


def solution(mesh):
    in_specs = (
        P("fsdp", "sp", None),
        P("fsdp", "sp", None),
        P(None, "fsdp", "sp"),
        P(None, "fsdp", None),
        P(None, None, "sp"),
        P("sp", "fsdp"),
        P("sp", None),
        P(None, "fsdp"),
        P(),
        P("fsdp"),
    )
    out_specs = (P("fsdp", "sp", None), P("fsdp", "sp", None))
    return jax.shard_map(
        per_device, mesh=mesh, in_specs=in_specs, out_specs=out_specs, check_vma=False
    )
```

profile of v0, /device:TPU:0, one launch (start us, length us, event | category | flops | bytes accessed | tf_op | source)
XLA Modules:
  0.0 461.0 jit_solution(10884928214685800891)
XLA Ops:
  7.3 1.0 copy-done
  8.2 3.4 add_convert_fusion
  11.7 1.2 fusion.7
  13.8 1.0 dynamic-slice_add_fusion.1
  15.0 2.1 all_gather.10
  17.1 298.8 %all-gather.3.cloned.1.call-done = bf16[3,3072,1536]{2,1,0:T(8,128)(2,1)} async-done(((bf16[3,192,1536]{2,1,0:T(8,128)(2,1)}), bf16[3,3072,1536]{2,1,0:T(8,128)(2,1)}) %all-gather.3.cloned.1.call-update) | async-done | bytes 28311568 | tf_op jit(solution)/shard_map/all_gather | solution.py:49
  315.8 11.7 %fusion.8 = bf16[3,48,1536]{2,1,0:T(8,128)(2,1)S(1)} fusion(bf16[3,3072,1536]{2,1,0:T(8,128)(2,1)} %all-gather.3.cloned.1.call-done, bf16[48,3072]{1,0:T(8,128)(2,1)S(1)} %all_gather.10), kind=kOutput, calls=%fused_computation.19 | convolution fusion | flops 1359175680 | bytes 29048832 | tf_op jit(solution)/shard_map/lr,prc->plc/dot_general | solution.py:46
  327.6 0.3 reshape.51
  328.0 4.7 %while.10 = (s32[]{:T(128)}, bf16[12,48,128]{2,1,0:T(8,128)(2,1)S(1)}, bf16[12,3,48,128]{3,2,1,0:T(8,128)(2,1)S(1)}, s32[]{:T(128)}, s32[]{:T(128)}, /*index=5*/s32[]{}, s32[]{}) while((s32[]{:T(128)}, bf16[12,48,128]{2,1,0:T(8,128)(2,1)S(1)}, bf16[12,3,48,128]{3,2,1,0:T(8,128)(2,1)S(1)}, s32[]{:T(128)}, s32[]{:T(128)}, /*index=5*/s32[]{}, ...), condition=%wide.region_4.5_spmd, body=%wide.region_1.4_spmd.sunk | while | flops 1201828 | bytes 95917 | solution.py:64
  328.2 0.2 fusion.33
  328.6 0.2 fusion.33
  329.0 0.2 fusion.33
  329.4 0.2 fusion.33
  329.8 0.2 fusion.33
  330.1 0.2 fusion.33
  330.5 0.2 fusion.33
  330.9 0.2 fusion.33
  331.3 0.2 fusion.33
  331.7 0.2 fusion.33
  332.1 0.2 fusion.33
  332.7 106.7 %all-gather.5.cloned.1.call-done = bf16[1536,3072]{0,1:T(8,128)(2,1)} async-done(((bf16[1536,192]{0,1:T(8,128)(2,1)}), bf16[1536,3072]{0,1:T(8,128)(2,1)}) %all-gather.5.cloned.1.call-update) | async-done | bytes 9437200 | tf_op jit(solution)/shard_map/all_gather | solution.py:69
  439.4 7.3 %convolution_convert_fusion.1 = bf16[48,3072]{1,0:T(8,128)(2,1)} fusion(bf16[1536,3072]{0,1:T(8,128)(2,1)} %all-gather.5.cloned.1.call-done, bf16[12,48,128]{2,1,0:T(8,128)(2,1)S(1)} %get-tuple-element.19), kind=kOutput, calls=%fused_computation.15 | convolution fusion | flops 453132288 | bytes 9879552 | tf_op jit(solution)/shard_map/dot_general | solution.py:71
  446.9 5.9 %reduce-scatter.2.cloned.1.call-done = bf16[24,3072]{1,0:T(8,128)(2,1)} async-done(((bf16[48,3072]{1,0:T(8,128)(2,1)}), bf16[24,3072]{1,0:T(8,128)(2,1)}) %reduce-scatter.2.cloned.1.call-update) | async-done | bytes 147472 | tf_op jit(solution)/shard_map/reduce_scatter | solution.py:70
  452.8 1.7 fusion.16
  (47 shorter events, 3.0 us)
Async XLA Ops:
  7.2 1.1 copy-start
  7.2 4.5 copy-start.2
  7.2 4.5 copy-start.3
  7.2 4.5 copy-start.5
  7.2 6.4 %copy-start.1 = (bf16[1,24,3072]{2,1,0:T(8,128)(2,1)S(1)}, bf16[1,24,3072]{2,1,0:T(8,128)(2,1)}, u32[]{:S(2)}) copy-start(bf16[1,24,3072]{2,1,0:T(8,128)(2,1)} %param.12) | copy-start | bytes 442372
  7.2 308.6 %all-gather.3.cloned.1.call-start = ((), (), s32[]{:S(2)}) async-start(), calls=%async_computation.1 | async-start | bytes 30081024 | tf_op jit(solution)/shard_map/all_gather | solution.py:49
  11.7 427.8 %all-gather.5.cloned.1.call-start = ((), (), s32[]{:S(2)}) async-start(), calls=%async_computation.2 | async-start | bytes 10027008 | tf_op jit(solution)/shard_map/all_gather | solution.py:69
  12.9 439.8 %reduce-scatter.2.cloned.1.call-start = ((), (), s32[]{:S(2)}) async-start(), calls=%async_computation.3 | async-start | bytes 442368 | tf_op jit(solution)/shard_map/reduce_scatter | solution.py:70
  439.4 13.3 %copy-start.4 = (bf16[1,24,3072]{2,1,0:T(8,128)(2,1)S(1)}, bf16[1,24,3072]{2,1,0:T(8,128)(2,1)}, u32[]{:S(2)}) copy-start(bf16[1,24,3072]{2,1,0:T(8,128)(2,1)} %param.13) | copy-start | bytes 442372
Sparse Core Ops, SparseCore 0:
  11.8 304.0 all-gather.2
  318.6 120.7 all-gather.4
  446.8 5.8 reduce-scatter.1
where the time goes:
time: 461 us
  waiting for transfers between devices  411 us (89%)
  matrix products  27.8 us (6%)
  between operations  14.6 us (3%)
    all_gather x1, waiting for transfers between devices, per_device(): lax.all_gather(merged_qkv, 'fsdp', axis=1, tiled=True)  299 us
    all_gather x1, waiting for transfers between devices, per_device(): full_out = lax.all_gather(merged_out, 'fsdp', axis=1, tiled=True)  107 us
    dot_general x1, matrix products, per_device(): jnp.einsum('lr,prc->plc', every_token, lax.all_gather(merged_qkv, 'fsdp',...  11.7 us
  transfers between devices with their start and end apart: 3, of which 3 were waited for; matrix products, arithmetic and copies ran while one was open for 4% of the time, Pallas kernels for 0%

commit v1 on v0

--- a/solution.py
+++ b/solution.py
@@ -1,6 +1,10 @@
+import functools
+
 import jax
 import jax.numpy as jnp
 from jax import lax
+from jax.experimental import pallas as pl
+from jax.experimental.pallas import tpu as pltpu
 from jax.sharding import PartitionSpec as P
 
 HEAD_DIM = 128
@@ -17,7 +21,376 @@
     return SHIFT_FACTOR * ramp / (1.0 + (SHIFT_FACTOR - 1.0) * ramp)
 
 
-def per_device(
+PLANE = 4
+MESH = pl.DeviceIdType.MESH
+
+
+def plane_kernel(
+    n_z,
+    step_ref,
+    latents_ref,
+    noise_ref,
+    base_qkv_ref,
+    down_qkv_ref,
+    up_qkv_ref,
+    base_out_ref,
+    down_out_ref,
+    up_out_ref,
+    mod_ref,
+    velocity_ref,
+    next_ref,
+    latf,
+    normed,
+    acts,
+    w_send,
+    w_recv,
+    part_send,
+    part_recv,
+    part_own,
+    att_send,
+    att_all,
+    wo_all,
+    out_half,
+    out_sib,
+    vel_send,
+    vel_recv,
+    lat_sem,
+    x1_sem,
+    x3_sem,
+    xs_sem,
+    w_sem,
+    p_sem,
+    wo_sem,
+    at_sem,
+    ag_sem,
+    os_sem,
+    v_sem,
+):
+    f, c = lax.axis_index("fsdp"), lax.axis_index("sp")
+    z, j = f // PLANE, f % PLANE
+    rows, d_model = latents_ref.shape
+    tokens = 2 * rows
+    n_head = w_send.shape[0]
+    block = d_model // n_z
+    half = block // 2
+    w_rows = base_qkv_ref.shape[1]
+    width = 3 * HEAD_DIM
+    f32, bf16 = jnp.float32, jnp.bfloat16
+
+    def in_plane(d):
+        return (z * PLANE + (j + d) % PLANE, c)
+
+    def in_column(d):
+        return (((z + d) % n_z) * PLANE + j, c)
+
+    sibling = (f, 1 - c)
+
+    def send(src, dst, sems, where, device):
+        copy = pltpu.make_async_remote_copy(
+            src_ref=src,
+            dst_ref=dst,
+            send_sem=sems.at[(0, *where)],
+            recv_sem=sems.at[(1, *where)],
+            device_id=device,
+            device_id_type=MESH,
+        )
+        copy.start()
+        return copy
+
+    started = []
+    barrier = pltpu.get_barrier_semaphore()
+    partners = [sibling]
+    partners += [in_plane(d) for d in range(1, PLANE)]
+    partners += [in_column(d) for d in range(1, n_z)]
+    for partner in partners:
+        pl.semaphore_signal(barrier, inc=1, device_id=partner, device_id_type=MESH)
+
+    latf[c] = latents_ref[...].astype(f32)
+    for p in range(3):
+        merged = (
+            base_qkv_ref[p].astype(f32)
+            + jnp.dot(down_qkv_ref[p], up_qkv_ref[p], preferred_element_type=f32)
+        ).astype(bf16)
+        for g in range(PLANE):
+            for h in range(n_head):
+                at = (g * n_head + h) * HEAD_DIM
+                w_send[h, g, :, p * HEAD_DIM : (p + 1) * HEAD_DIM] = merged[:, at : at + HEAD_DIM]
+    pl.semaphore_wait(barrier, len(partners))
+
+    lat_copy = send(latf.at[c], latf.at[c], lat_sem, (), sibling)
+    w_copies = {}
+
+    def send_weights(h):
+        for d in range(1, PLANE):
+            w_copies[h, d] = send(
+                w_send.at[h, (j + d) % PLANE], w_recv.at[h, j], w_sem, (h, d - 1), in_plane(d)
+            )
+
+    send_weights(0)
+    for h in range(n_head):
+        w_recv[h, j] = w_send[h, j]
+
+    step_index = step_ref[0]
+    mod_rows = mod_ref[step_index]
+    lat_copy.wait_recv()
+    lat_rows = latf[...].reshape(tokens, d_model)
+    mean_square = jnp.mean(lat_rows * lat_rows, axis=-1, keepdims=True)
+    normed[...] = (
+        lat_rows * lax.rsqrt(mean_square + EPSILON) * (1.0 + mod_rows[1:2]) + mod_rows[0:1]
+    ).astype(bf16)
+
+    def features(z_at):
+        return pl.ds(pl.multiple_of(z_at * block + c * half, half), half)
+
+    x1 = [
+        send(
+            normed.at[:, features((z + d) % n_z)],
+            acts.at[c, z, j],
+            x1_sem,
+            (d - 1,),
+            in_column(d),
+        )
+        for d in range(1, n_z)
+    ]
+    acts[c, z, j] = normed[:, features(z)]
+    for copy in x1:
+        copy.wait_recv()
+    x3 = [
+        send(acts.at[c, :, j], acts.at[c, :, j], x3_sem, (d - 1,), in_plane(d))
+        for d in range(1, PLANE)
+    ]
+    xs = [send(acts.at[c, :, j], acts.at[c, :, j], xs_sem, (0,), sibling)]
+    for h in range(1, n_head):
+        send_weights(h)
+    merged_out = (
+        base_out_ref[...].astype(f32).T
+        + lax.dot_general(
+            up_out_ref[...],
+            down_out_ref[...],
+            (((0,), (1,)), ((), ())),
+            preferred_element_type=f32,
+        )
+    ).astype(bf16)
+    for g in range(PLANE):
+        for h in range(n_head):
+            at, to = (g * n_head + h) * HEAD_DIM, (h * PLANE + g) * HEAD_DIM
+            wo_all[j, :, to : to + HEAD_DIM] = merged_out[:, at : at + HEAD_DIM]
+    for d in range(1, PLANE):
+        x3[d - 1].wait_recv()
+        came = (j + PLANE - d) % PLANE
+        xs.append(send(acts.at[c, :, came], acts.at[c, :, came], xs_sem, (d,), sibling))
+    wo = [
+        send(wo_all.at[j], wo_all.at[j], wo_sem, (d - 1,), in_plane(d)) for d in range(1, PLANE)
+    ]
+    for copy in xs:
+        copy.wait_recv()
+
+    p_copies = {}
+    for h in range(n_head):
+        for d in range(1, PLANE):
+            w_copies[h, d].wait_recv()
+        weights = w_recv[h].reshape(PLANE * w_rows, width)
+        for d in list(range(1, n_z)) + [0]:
+            z_at = (z + d) % n_z
+            part = jnp.dot(
+                acts[0, z_at].reshape(PLANE * tokens, half),
+                weights[:half],
+                preferred_element_type=f32,
+            ) + jnp.dot(
+                acts[1, z_at].reshape(PLANE * tokens, half),
+                weights[half:],
+                preferred_element_type=f32,
+            )
+            if d:
+                part_send[h, z_at] = part.astype(bf16)
+                p_copies[h, d] = send(
+                    part_send.at[h, z_at], part_recv.at[h, d - 1], p_sem, (h, d - 1), in_column(d)
+                )
+            else:
+                part_own[h] = part
+
+    at_copies, ag_copies = {}, {}
+
+    def lanes(h, g):
+        return pl.ds(pl.multiple_of((h * PLANE + g) * HEAD_DIM, HEAD_DIM), HEAD_DIM)
+
+    def spread(h):
+        for d in range(1, PLANE):
+            at_copies[h, d].wait_recv()
+        chunk = pl.ds(h * PLANE * HEAD_DIM, PLANE * HEAD_DIM)
+        for d in range(1, n_z):
+            ag_copies[h, d] = send(
+                att_all.at[z, :, chunk],
+                att_all.at[z, :, chunk],
+                ag_sem,
+                (h, d - 1),
+                in_column(d),
+            )
+
+    for h in range(n_head):
+        total = part_own[h]
+        for d in range(1, n_z):
+            p_copies[h, d].wait_recv()
+            total = total + part_recv[h, d - 1].astype(f32)
+        projected = total.astype(bf16)
+        for s in range(PLANE):
+            rows_s = projected[s * tokens : (s + 1) * tokens]
+            query = rows_s[:, :HEAD_DIM]
+            key = rows_s[:, HEAD_DIM : 2 * HEAD_DIM]
+            value = rows_s[:, 2 * HEAD_DIM :]
+            scores = lax.dot_general(
+                query, key, (((1,), (1,)), ((), ())), preferred_element_type=f32
+            ) * (1.0 / HEAD_DIM**0.5)
+            weights = jnp.exp(scores - jnp.max(scores, axis=-1, keepdims=True))
+            weights = weights / jnp.sum(weights, axis=-1, keepdims=True)
+            att_send[h, s] = jnp.dot(
+                weights.astype(bf16), value, preferred_element_type=f32
+            ).astype(bf16)
+        for d in range(1, PLANE):
+            at_copies[h, d] = send(
+                att_send.at[h, (j + d) % PLANE],
+                att_all.at[z, :, lanes(h, j)],
+                at_sem,
+                (h, d - 1),
+                in_plane(d),
+            )
+        att_all[z, :, lanes(h, j)] = att_send[h, j]
+        if h:
+            spread(h - 1)
+    spread(n_head - 1)
+
+    for copy in wo:
+        copy.wait_recv()
+    for copy in ag_copies.values():
+        copy.wait_recv()
+    out = lax.dot_general(
+        att_all[...].reshape(n_z * tokens, att_all.shape[2]),
+        wo_all[...].reshape(block, att_all.shape[2]),
+        (((1,), (1,)), ((), ())),
+        preferred_element_type=f32,
+    )
+    for s in range(n_z):
+        for k in range(2):
+            at = s * tokens + k * rows
+            out_half[k, s] = out[at : at + rows]
+    os_copy = send(out_half.at[1 - c], out_sib, os_sem, (), sibling)
+    os_copy.wait_recv()
+    pad = jnp.zeros((vel_send.shape[1] - rows, block), f32)
+    v_copies = []
+    for d in list(range(1, n_z)) + [0]:
+        z_at = (z + d) % n_z
+        block_sum = out_half[c, z_at] + out_sib[z_at]
+        block_sum = jnp.concatenate([block_sum, pad], axis=0).astype(bf16)
+        if d:
+            vel_send[z_at] = block_sum
+            v_copies.append(
+                send(vel_send.at[z_at], vel_recv.at[z], v_sem, (d - 1,), in_column(d))
+            )
+        else:
+            vel_recv[z] = block_sum
+
+    position = jnp.full((1, block), step_index.astype(f32), f32)
+    step_size = plan_sigma(position + 1.0) - plan_sigma(position)
+    noise_size = NOISE_LEVEL * jnp.sqrt(-step_size)
+    for copy in v_copies:
+        copy.wait_recv()
+    for s in range(n_z):
+        cols = slice(s * block, (s + 1) * block)
+        block_out = vel_recv[s].astype(f32)[:rows]
+        velocity = ((1.0 + mod_rows[2:3, cols]) * block_out).astype(bf16)
+        velocity_ref[:, cols] = velocity
+        next_ref[:, cols] = (
+            latf[c, :, cols]
+            + step_size * velocity.astype(f32)
+            + noise_size * noise_ref[:, cols].astype(f32)
+        ).astype(bf16)
+
+    every = [lat_copy, os_copy, *x1, *x3, *xs, *wo, *v_copies]
+    for group in (w_copies, p_copies, at_copies, ag_copies):
+        every += list(group.values())
+    for copy in every:
+        copy.wait_send()
+
+
+def per_device(*args):
+    latents, step_noise, base_qkv, down_qkv, up_qkv, base_out, down_out, up_out, modulation, step = (
+        args
+    )
+    n_fsdp, n_sp = lax.axis_size("fsdp"), lax.axis_size("sp")
+    _, rows, d_model = latents.shape
+    heads_here = base_qkv.shape[2] // HEAD_DIM
+    tokens = rows * n_sp
+    if n_sp != 2 or n_fsdp % PLANE or heads_here % PLANE or tokens % 16:
+        return gather_weights(*args)
+    n_z, n_head = n_fsdp // PLANE, heads_here // PLANE
+    block = d_model // n_z
+    half = block // 2
+    w_rows = base_qkv.shape[1]
+    width = 3 * HEAD_DIM
+    cols = base_qkv.shape[2]
+    f32, bf16 = jnp.float32, jnp.bfloat16
+    if half % HEAD_DIM or w_rows % 16 or block != PLANE * w_rows or base_out.shape[1] != w_rows:
+        return gather_weights(*args)
+    padded = -(-rows // 16) * 16
+    dma = pltpu.SemaphoreType.DMA
+    vmem = pl.BlockSpec(memory_space=pltpu.VMEM)
+    velocity, next_rows = pl.pallas_call(
+        functools.partial(plane_kernel, n_z),
+        out_shape=[jax.ShapeDtypeStruct((rows, d_model), bf16)] * 2,
+        in_specs=[pl.BlockSpec(memory_space=pltpu.SMEM)] + [vmem] * 9,
+        out_specs=[vmem] * 2,
+        scratch_shapes=[
+            pltpu.VMEM((2, rows, d_model), f32),
+            pltpu.VMEM((tokens, d_model), bf16),
+            pltpu.VMEM((2, n_z, PLANE, tokens, half), bf16),
+            pltpu.VMEM((n_head, PLANE, w_rows, width), bf16),
+            pltpu.VMEM((n_head, PLANE, w_rows, width), bf16),
+            pltpu.VMEM((n_head, n_z, PLANE * tokens, width), bf16),
+            pltpu.VMEM((n_head, n_z - 1, PLANE * tokens, width), bf16),
+            pltpu.VMEM((n_head, PLANE * tokens, width), f32),
+            pltpu.VMEM((n_head, PLANE, tokens, HEAD_DIM), bf16),
+            pltpu.VMEM((n_z, tokens, cols), bf16),
+            pltpu.VMEM((PLANE, w_rows, cols), bf16),
+            pltpu.VMEM((2, n_z, rows, block), f32),
+            pltpu.VMEM((n_z, rows, block), f32),
+            pltpu.VMEM((n_z, padded, block), bf16),
+            pltpu.VMEM((n_z, padded, block), bf16),
+            dma((2,)),
+            dma((2, n_z - 1)),
+            dma((2, PLANE - 1)),
+            dma((2, PLANE)),
+            dma((2, n_head, PLANE - 1)),
+            dma((2, n_head, n_z - 1)),
+            dma((2, PLANE - 1)),
+            dma((2, n_head, PLANE - 1)),
+            dma((2, n_head, n_z - 1)),
+            dma((2,)),
+            dma((2, n_z - 1)),
+        ],
+        compiler_params=pltpu.CompilerParams(
+            collective_id=0, has_side_effects=True, vmem_limit_bytes=48 * 1024 * 1024
+        ),
+        cost_estimate=pl.CostEstimate(
+            flops=2 * n_fsdp * tokens * w_rows * 4 * cols,
+            bytes_accessed=8 * w_rows * cols,
+            transcendentals=0,
+        ),
+    )(
+        step,
+        latents[0],
+        step_noise[0],
+        base_qkv,
+        down_qkv,
+        up_qkv,
+        base_out,
+        down_out,
+        up_out,
+        modulation,
+    )
+    return (velocity[None], next_rows[None])
+
+
+def gather_weights(
     latents,
     step_noise,
     base_qkv,

time: 461 us -> 91.6 us (0.20)
  waiting for transfers between devices: 411 us -> 0 us
  Pallas kernels: 0 us -> 82.3 us
  matrix products: 27.8 us -> 0 us
  between operations: 14.6 us -> 1.37 us
  local copies, waits for them, and re-layouts: 1.43 us -> 7.56 us
    all_gather x2 -> x0, waiting for transfers between devices: 405 us -> none  [the longest x1 299 us: per_device(): lax.all_gather(merged_qkv, 'fsdp', axis=1, tiled=True)]
    pallas_call x0 -> x1, Pallas kernels: none -> 82.3 us  [per_device(): pl.pallas_call(functools.partial(plane_kernel, n_z), out_shape=[jax.Shape...]
    dot_general x28 -> x0, matrix products: 27.8 us -> none  [the longest x1 11.7 us: per_device(): jnp.einsum('lr,prc->plc', every_token, lax.all_gather(merged_qkv, 'fsdp',...]
    unnamed x12 -> x16, local copies, waits for them, and re-layouts: 1 us -> 7.56 us
    reduce_scatter x1 -> x0, waiting for transfers between devices: 5.9 us -> none  [per_device(): lax.psum_scatter(jnp.dot(attention_result, full_out, preferred_element_ty...]
  transfers between devices with their start and end apart: 3 -> 0, of which waited for: 3 -> 0; matrix products, arithmetic and copies ran while one was open for 4% -> 0% of each run, Pallas kernels for 0% -> 0%
where the time goes in v1:
time: 91.6 us; the launch traced here: 91.3 us
  Pallas kernels  82.3 us (90%)
  local copies, waits for them, and re-layouts  7.56 us (8%)
  between operations  1.37 us (1%)
    pallas_call x1, Pallas kernels, per_device(): pl.pallas_call(functools.partial(plane_kernel, n_z), out_shape=[jax.Shape...  82.3 us
    unnamed x16, local copies, waits for them, and re-layouts  7.56 us

profile of v1, /device:TPU:0, one launch (start us, length us, event | category | flops | bytes accessed | tf_op | source)
XLA Modules:
  0.0 91.3 jit_solution(7351805715979707174)
XLA Ops:
  1.3 0.0 copy-start
  1.3 0.0 copy-start.2
  1.3 0.0 copy-start.3
  1.3 0.0 copy-start.4
  1.3 1.2 %copy.12.down_qkv_ref = bf16[3,192,64]{2,1,0:T(8,128)(2,1)S(1)} copy(bf16[3,192,64]{1,2,0:T(8,128)(2,1)} %param.13) | data formatting | bytes 147456 | tf_op args[3]
  2.5 1.2 %copy.14.down_out_ref = bf16[1536,64]{1,0:T(8,128)(2,1)S(1)} copy(bf16[1536,64]{0,1:T(8,128)(2,1)} %param.16) | data formatting | bytes 393216 | tf_op args[6]
  3.7 1.3 %copy.13.base_out_ref = bf16[1536,192]{1,0:T(8,128)(2,1)S(1)} copy(bf16[1536,192]{0,1:T(8,128)(2,1)} %param.15) | data formatting | bytes 1179648 | tf_op args[5]
  5.0 1.5 %copy.15.mod_ref = f32[16,3,3072]{2,1,0:T(4,128)S(1)} copy(f32[16,3,3072]{2,0,1:T(8,128)} %param.18) | data formatting | bytes 1179648 | tf_op args[8]
  6.5 0.0 copy-done
  6.5 0.0 copy-done.2
  6.5 0.0 copy-done.3
  6.5 0.0 copy-done.4
  6.5 0.0 copy-start.1
  6.5 1.1 %copy-done.1 = bf16[3,64,1536]{2,1,0:T(8,128)(2,1)S(1)} copy-done((bf16[3,64,1536]{2,1,0:T(8,128)(2,1)S(1)}, bf16[3,64,1536]{2,1,0:T(8,128)(2,1)}, u32[]{:S(2)}) %copy-start.1) | copy-done | bytes 589848
  7.6 82.3 %shard_map.113 = (bf16[24,3072]{1,0:T(8,128)(2,1)S(1)}, bf16[24,3072]{1,0:T(8,128)(2,1)S(1)}) custom-call(s32[1]{0:T(128)S(6)} %copy.18.step_ref, bf16[24,3072]{1,0:T(8,128)(2,1)S(1)} %bitcast.6, bf16[24,3072]{1,0:T(8,128)(2,1)S(1)} %bitcast.7, bf16[3,192,1536]{2,1,0:T(8,128)(2,1)S(1)} %copy-done, bf16[3,192,64]{2,1,0:T(8,128)(2,1)S(1)} %copy.12.down_qkv_ref, ...), custom_call_target="tpu_custom_call" | custom-call | flops 1811939328 | bytes 2359296 | tf_op jit(solution)/shard_map/pallas_call | solution.py:337
  89.9 0.7 copy.19
  90.6 0.7 copy.20
Async XLA Ops:
  1.3 5.2 %copy-start = (bf16[3,192,1536]{2,1,0:T(8,128)(2,1)S(1)}, bf16[3,192,1536]{2,1,0:T(8,128)(2,1)}, u32[]{:S(2)}) copy-start(bf16[3,192,1536]{2,1,0:T(8,128)(2,1)} %base_qkv_ref.1) | copy-start | bytes 5308420
  1.3 5.2 %copy-start.2 = (bf16[1,24,3072]{2,1,0:T(8,128)(2,1)S(1)}, bf16[1,24,3072]{2,1,0:T(8,128)(2,1)}, u32[]{:S(2)}) copy-start(bf16[1,24,3072]{2,1,0:T(8,128)(2,1)} %param.10) | copy-start | bytes 442372
  1.3 5.2 %copy-start.3 = (bf16[1,24,3072]{2,1,0:T(8,128)(2,1)S(1)}, bf16[1,24,3072]{2,1,0:T(8,128)(2,1)}, u32[]{:S(2)}) copy-start(bf16[1,24,3072]{2,1,0:T(8,128)(2,1)} %param.11) | copy-start | bytes 442372
  1.3 5.2 %copy-start.4 = (bf16[64,192]{1,0:T(8,128)(2,1)S(1)}, bf16[64,192]{1,0:T(8,128)(2,1)}, u32[]{:S(2)}) copy-start(bf16[64,192]{1,0:T(8,128)(2,1)} %up_out_ref.1) | copy-start | bytes 73732
  6.5 1.1 %copy-start.1 = (bf16[3,64,1536]{2,1,0:T(8,128)(2,1)S(1)}, bf16[3,64,1536]{2,1,0:T(8,128)(2,1)}, u32[]{:S(2)}) copy-start(bf16[3,64,1536]{2,1,0:T(8,128)(2,1)} %up_qkv_ref.1) | copy-start | bytes 1769476

commit v2 on v1

--- a/solution.py
+++ b/solution.py
@@ -59,7 +59,8 @@
     x3_sem,
     xs_sem,
     w_sem,
-    p_sem,
+    pair_sem,
+    far_sem,
     wo_sem,
     at_sem,
     ag_sem,
@@ -74,6 +75,9 @@
     block = d_model // n_z
     half = block // 2
     w_rows = base_qkv_ref.shape[1]
+    x_at, y_at = j % 2, j // 2
+    z_lo, z_hi = z % 2, z // 2
+    x_near, y_near = 2 * y_at + 1 - x_at, 2 * (1 - y_at) + x_at
     width = 3 * HEAD_DIM
     f32, bf16 = jnp.float32, jnp.bfloat16
 
@@ -84,6 +88,9 @@
         return (((z + d) % n_z) * PLANE + j, c)
 
     sibling = (f, 1 - c)
+    x_device, y_device = (z * PLANE + x_near, c), (z * PLANE + y_near, c)
+    z_pair = ((2 * z_hi + 1 - z_lo) * PLANE + j, c)
+    z_far = ((2 * (1 - z_hi) + z_lo) * PLANE + j, c)
 
     def send(src, dst, sems, where, device):
         copy = pltpu.make_async_remote_copy(
@@ -97,7 +104,6 @@
         copy.start()
         return copy
 
-    started = []
     barrier = pltpu.get_barrier_semaphore()
     partners = [sibling]
     partners += [in_plane(d) for d in range(1, PLANE)]
@@ -106,17 +112,23 @@
         pl.semaphore_signal(barrier, inc=1, device_id=partner, device_id_type=MESH)
 
     latf[c] = latents_ref[...].astype(f32)
-    for p in range(3):
-        merged = (
-            base_qkv_ref[p].astype(f32)
-            + jnp.dot(down_qkv_ref[p], up_qkv_ref[p], preferred_element_type=f32)
-        ).astype(bf16)
+
+    def merge(h):
         for g in range(PLANE):
-            for h in range(n_head):
-                at = (g * n_head + h) * HEAD_DIM
-                w_send[h, g, :, p * HEAD_DIM : (p + 1) * HEAD_DIM] = merged[:, at : at + HEAD_DIM]
+            at = (g * n_head + h) * HEAD_DIM
+            for p in range(3):
+                lowrank = lax.dot_general(
+                    down_qkv_ref[p],
+                    up_qkv_ref[p, :, at : at + HEAD_DIM],
+                    (((0,), (0,)), ((), ())),
+                    preferred_element_type=f32,
+                )
+                w_send[h, g, :, p * HEAD_DIM : (p + 1) * HEAD_DIM] = (
+                    base_qkv_ref[p, :, at : at + HEAD_DIM].astype(f32) + lowrank
+                ).astype(bf16)
+        w_recv[h, j] = w_send[h, j]
+
     pl.semaphore_wait(barrier, len(partners))
-
     lat_copy = send(latf.at[c], latf.at[c], lat_sem, (), sibling)
     w_copies = {}
 
@@ -126,17 +138,19 @@
                 w_send.at[h, (j + d) % PLANE], w_recv.at[h, j], w_sem, (h, d - 1), in_plane(d)
             )
 
+    merge(0)
     send_weights(0)
-    for h in range(n_head):
-        w_recv[h, j] = w_send[h, j]
 
     step_index = step_ref[0]
-    mod_rows = mod_ref[step_index]
+
+    def mod_row(k):
+        return mod_ref[k, pl.ds(step_index, 1), :]
+
     lat_copy.wait_recv()
     lat_rows = latf[...].reshape(tokens, d_model)
     mean_square = jnp.mean(lat_rows * lat_rows, axis=-1, keepdims=True)
     normed[...] = (
-        lat_rows * lax.rsqrt(mean_square + EPSILON) * (1.0 + mod_rows[1:2]) + mod_rows[0:1]
+        lat_rows * lax.rsqrt(mean_square + EPSILON) * (1.0 + mod_row(1)) + mod_row(0)
     ).astype(bf16)
 
     def features(z_at):
@@ -153,6 +167,8 @@
         for d in range(1, n_z)
     ]
     acts[c, z, j] = normed[:, features(z)]
+    if n_head > 1:
+        merge(1)
     for copy in x1:
         copy.wait_recv()
     x3 = [
@@ -161,13 +177,15 @@
     ]
     xs = [send(acts.at[c, :, j], acts.at[c, :, j], xs_sem, (0,), sibling)]
     for h in range(1, n_head):
+        if h > 1:
+            merge(h)
         send_weights(h)
     merged_out = (
-        base_out_ref[...].astype(f32).T
+        base_out_ref[...].astype(f32)
         + lax.dot_general(
             up_out_ref[...],
             down_out_ref[...],
-            (((0,), (1,)), ((), ())),
+            (((0,), (0,)), ((), ())),
             preferred_element_type=f32,
         )
     ).astype(bf16)
@@ -179,19 +197,23 @@
         x3[d - 1].wait_recv()
         came = (j + PLANE - d) % PLANE
         xs.append(send(acts.at[c, :, came], acts.at[c, :, came], xs_sem, (d,), sibling))
-    wo = [
-        send(wo_all.at[j], wo_all.at[j], wo_sem, (d - 1,), in_plane(d)) for d in range(1, PLANE)
-    ]
     for copy in xs:
         copy.wait_recv()
 
-    p_copies = {}
+    wo_x, wo_y, wo_far = [], [], []
+    wo_half = w_rows // 2
+
+    def send_out_rows(owner, k, where, device):
+        view = wo_all.at[owner, pl.ds(k * wo_half, wo_half)]
+        return send(view, view, wo_sem, where, device)
+
+    pair_copies, far_copies = {}, {}
     for h in range(n_head):
         for d in range(1, PLANE):
             w_copies[h, d].wait_recv()
         weights = w_recv[h].reshape(PLANE * w_rows, width)
-        for d in list(range(1, n_z)) + [0]:
-            z_at = (z + d) % n_z
+        for parity, hi in ((1, 1), (1, 0), (0, 1), (0, 0)):
+            z_at = 2 * ((z_hi + hi) % 2) + (z_lo + parity) % 2
             part = jnp.dot(
                 acts[0, z_at].reshape(PLANE * tokens, half),
                 weights[:half],
@@ -201,13 +223,22 @@
                 weights[half:],
                 preferred_element_type=f32,
             )
-            if d:
-                part_send[h, z_at] = part.astype(bf16)
-                p_copies[h, d] = send(
-                    part_send.at[h, z_at], part_recv.at[h, d - 1], p_sem, (h, d - 1), in_column(d)
+            if parity:
+                part_send[h, hi] = part.astype(bf16)
+                pair_copies[h, hi] = send(
+                    part_send.at[h, hi], part_recv.at[h, hi], pair_sem, (h, hi), z_pair
                 )
             else:
-                part_own[h] = part
+                part_own[h, hi] = part
+        if h == min(1, n_head - 1):
+            for k in range(2):
+                wo_x.append(send_out_rows(j, k, (0, k), x_device))
+                wo_y.append(send_out_rows(j, 1 - k, (1, 1 - k), y_device))
+
+    def send_far(h):
+        pair_copies[h, 1].wait_recv()
+        part_send[h, 2] = (part_own[h, 1] + part_recv[h, 1].astype(f32)).astype(bf16)
+        far_copies[h] = send(part_send.at[h, 2], part_recv.at[h, 2], far_sem, (h,), z_far)
 
     at_copies, ag_copies = {}, {}
 
@@ -227,12 +258,12 @@
                 in_column(d),
             )
 
-    for h in range(n_head):
-        total = part_own[h]
-        for d in range(1, n_z):
-            p_copies[h, d].wait_recv()
-            total = total + part_recv[h, d - 1].astype(f32)
-        projected = total.astype(bf16)
+    def attend(h):
+        pair_copies[h, 0].wait_recv()
+        far_copies[h].wait_recv()
+        projected = (
+            part_own[h, 0] + part_recv[h, 0].astype(f32) + part_recv[h, 2].astype(f32)
+        ).astype(bf16)
         for s in range(PLANE):
             rows_s = projected[s * tokens : (s + 1) * tokens]
             query = rows_s[:, :HEAD_DIM]
@@ -255,20 +286,35 @@
                 in_plane(d),
             )
         att_all[z, :, lanes(h, j)] = att_send[h, j]
+
+    send_far(0)
+    for h in range(n_head):
+        if h + 1 < n_head:
+            send_far(h + 1)
+        else:
+            wo_x[0].wait_recv()
+            wo_far.append(send_out_rows(x_near, 0, (2, 0), y_device))
+            wo_y[0].wait_recv()
+            wo_far.append(send_out_rows(y_near, 1, (2, 1), x_device))
+        attend(h)
         if h:
             spread(h - 1)
     spread(n_head - 1)
 
-    for copy in wo:
+    for copy in (wo_x[1], wo_y[1], *wo_far):
         copy.wait_recv()
-    for copy in ag_copies.values():
-        copy.wait_recv()
-    out = lax.dot_general(
-        att_all[...].reshape(n_z * tokens, att_all.shape[2]),
-        wo_all[...].reshape(block, att_all.shape[2]),
-        (((1,), (1,)), ((), ())),
-        preferred_element_type=f32,
-    )
+    out = None
+    for h in range(n_head):
+        for d in range(1, n_z):
+            ag_copies[h, d].wait_recv()
+        chunk = slice(h * PLANE * HEAD_DIM, (h + 1) * PLANE * HEAD_DIM)
+        term = lax.dot_general(
+            att_all[:, :, chunk].reshape(n_z * tokens, PLANE * HEAD_DIM),
+            wo_all[:, :, chunk].reshape(block, PLANE * HEAD_DIM),
+            (((1,), (1,)), ((), ())),
+            preferred_element_type=f32,
+        )
+        out = term if out is None else out + term
     for s in range(n_z):
         for k in range(2):
             at = s * tokens + k * rows
@@ -289,6 +335,7 @@
         else:
             vel_recv[z] = block_sum
 
+    gate = mod_row(2)
     position = jnp.full((1, block), step_index.astype(f32), f32)
     step_size = plan_sigma(position + 1.0) - plan_sigma(position)
     noise_size = NOISE_LEVEL * jnp.sqrt(-step_size)
@@ -297,7 +344,7 @@
     for s in range(n_z):
         cols = slice(s * block, (s + 1) * block)
         block_out = vel_recv[s].astype(f32)[:rows]
-        velocity = ((1.0 + mod_rows[2:3, cols]) * block_out).astype(bf16)
+        velocity = ((1.0 + gate[:, cols]) * block_out).astype(bf16)
         velocity_ref[:, cols] = velocity
         next_ref[:, cols] = (
             latf[c, :, cols]
@@ -305,8 +352,8 @@
             + noise_size * noise_ref[:, cols].astype(f32)
         ).astype(bf16)
 
-    every = [lat_copy, os_copy, *x1, *x3, *xs, *wo, *v_copies]
-    for group in (w_copies, p_copies, at_copies, ag_copies):
+    every = [lat_copy, os_copy, *x1, *x3, *xs, *wo_x, *wo_y, *wo_far, *v_copies]
+    for group in (w_copies, pair_copies, far_copies, at_copies, ag_copies):
         every += list(group.values())
     for copy in every:
         copy.wait_send()
@@ -320,7 +367,7 @@
     _, rows, d_model = latents.shape
     heads_here = base_qkv.shape[2] // HEAD_DIM
     tokens = rows * n_sp
-    if n_sp != 2 or n_fsdp % PLANE or heads_here % PLANE or tokens % 16:
+    if n_sp != 2 or n_fsdp != 4 * PLANE or heads_here % PLANE or tokens % 16:
         return gather_weights(*args)
     n_z, n_head = n_fsdp // PLANE, heads_here // PLANE
     block = d_model // n_z
@@ -329,7 +376,7 @@
     width = 3 * HEAD_DIM
     cols = base_qkv.shape[2]
     f32, bf16 = jnp.float32, jnp.bfloat16
-    if half % HEAD_DIM or w_rows % 16 or block != PLANE * w_rows or base_out.shape[1] != w_rows:
+    if half % HEAD_DIM or w_rows % 32 or block != PLANE * w_rows or base_out.shape[1] != w_rows:
         return gather_weights(*args)
     padded = -(-rows // 16) * 16
     dma = pltpu.SemaphoreType.DMA
@@ -345,9 +392,9 @@
             pltpu.VMEM((2, n_z, PLANE, tokens, half), bf16),
             pltpu.VMEM((n_head, PLANE, w_rows, width), bf16),
             pltpu.VMEM((n_head, PLANE, w_rows, width), bf16),
-            pltpu.VMEM((n_head, n_z, PLANE * tokens, width), bf16),
-            pltpu.VMEM((n_head, n_z - 1, PLANE * tokens, width), bf16),
-            pltpu.VMEM((n_head, PLANE * tokens, width), f32),
+            pltpu.VMEM((n_head, 3, PLANE * tokens, width), bf16),
+            pltpu.VMEM((n_head, 3, PLANE * tokens, width), bf16),
+            pltpu.VMEM((n_head, 2, PLANE * tokens, width), f32),
             pltpu.VMEM((n_head, PLANE, tokens, HEAD_DIM), bf16),
             pltpu.VMEM((n_z, tokens, cols), bf16),
             pltpu.VMEM((PLANE, w_rows, cols), bf16),
@@ -360,8 +407,9 @@
             dma((2, PLANE - 1)),
             dma((2, PLANE)),
             dma((2, n_head, PLANE - 1)),
-            dma((2, n_head, n_z - 1)),
-            dma((2, PLANE - 1)),
+            dma((2, n_head, 2)),
+            dma((2, n_head)),
+            dma((2, 3, 2)),
             dma((2, n_head, PLANE - 1)),
             dma((2, n_head, n_z - 1)),
             dma((2,)),
@@ -380,12 +428,12 @@
         latents[0],
         step_noise[0],
         base_qkv,
-        down_qkv,
+        down_qkv.swapaxes(1, 2),
         up_qkv,
-        base_out,
-        down_out,
+        base_out.T,
+        down_out.T,
         up_out,
-        modulation,
+        modulation.swapaxes(0, 1),
     )
     return (velocity[None], next_rows[None])
 

time: 91.6 us -> 89 us (0.972)
  Pallas kernels: 82.3 us -> 76.9 us
  local copies, waits for them, and re-layouts: 7.56 us -> 10.4 us
    pallas_call x1, Pallas kernels: 82.3 us -> 76.9 us  [per_device(): pl.pallas_call(functools.partial(plane_kernel, n_z), out_shape=[jax.Shape...]
    unnamed x16 -> x20, local copies, waits for them, and re-layouts: 7.56 us -> 10.4 us
where the time goes in v2:
time: 89 us; the launch traced here: 88.6 us
  Pallas kernels  76.9 us (86%)
  local copies, waits for them, and re-layouts  10.4 us (12%)
  between operations  1.31 us (1%)
    pallas_call x1, Pallas kernels, per_device(): pl.pallas_call(functools.partial(plane_kernel, n_z), out_shape=[jax.Shape...  76.9 us
    unnamed x20, local copies, waits for them, and re-layouts  10.4 us

profile of v2, /device:TPU:0, one launch (start us, length us, event | category | flops | bytes accessed | tf_op | source)
XLA Modules:
  0.0 88.6 jit_solution(13636407575237975678)
XLA Ops:
  1.3 0.0 copy-start
  1.3 1.5 %copy-done = bf16[3,192,1536]{2,1,0:T(8,128)(2,1)S(1)} copy-done((bf16[3,192,1536]{2,1,0:T(8,128)(2,1)S(1)}, bf16[3,192,1536]{2,1,0:T(8,128)(2,1)}, u32[]{:S(2)}) %copy-start) | copy-done | bytes 1769496
  2.8 0.0 copy-start.1
  2.8 1.1 %copy-done.1 = bf16[3,64,1536]{2,1,0:T(8,128)(2,1)S(1)} copy-done((bf16[3,64,1536]{2,1,0:T(8,128)(2,1)S(1)}, bf16[3,64,1536]{2,1,0:T(8,128)(2,1)}, u32[]{:S(2)}) %copy-start.1) | copy-done | bytes 589848
  3.8 0.0 copy-start.2
  3.8 1.1 %copy-done.2 = bf16[1536,192]{0,1:T(8,128)(2,1)S(1)} copy-done((bf16[1536,192]{0,1:T(8,128)(2,1)S(1)}, bf16[1536,192]{0,1:T(8,128)(2,1)}, u32[]{:S(2)}) %copy-start.2) | copy-done | bytes 589848
  4.9 0.0 copy-start.3
  4.9 1.1 %copy-done.3 = f32[16,3,3072]{2,0,1:T(8,128)S(1)} copy-done((f32[16,3,3072]{2,0,1:T(8,128)S(1)}, f32[16,3,3072]{2,0,1:T(8,128)}, u32[]{:S(2)}) %copy-start.3) | copy-done | bytes 589848
  6.0 0.0 copy-start.4
  6.0 0.9 %copy-done.4 = bf16[1536,64]{0,1:T(8,128)(2,1)S(1)} copy-done((bf16[1536,64]{0,1:T(8,128)(2,1)S(1)}, bf16[1536,64]{0,1:T(8,128)(2,1)}, u32[]{:S(2)}) %copy-start.4) | copy-done | bytes 196632
  6.9 0.0 copy-start.5
  6.9 0.9 %copy-done.5 = bf16[1,24,3072]{2,1,0:T(8,128)(2,1)S(1)} copy-done((bf16[1,24,3072]{2,1,0:T(8,128)(2,1)S(1)}, bf16[1,24,3072]{2,1,0:T(8,128)(2,1)}, u32[]{:S(2)}) %copy-start.5) | copy-done | bytes 147480
  7.8 0.0 copy-start.6
  7.8 0.9 %copy-done.6 = bf16[1,24,3072]{2,1,0:T(8,128)(2,1)S(1)} copy-done((bf16[1,24,3072]{2,1,0:T(8,128)(2,1)S(1)}, bf16[1,24,3072]{2,1,0:T(8,128)(2,1)}, u32[]{:S(2)}) %copy-start.6) | copy-done | bytes 147480
  8.7 0.0 copy-start.7
  8.7 0.9 %copy-done.7 = bf16[3,192,64]{1,2,0:T(8,128)(2,1)S(1)} copy-done((bf16[3,192,64]{1,2,0:T(8,128)(2,1)S(1)}, bf16[3,192,64]{1,2,0:T(8,128)(2,1)}, u32[]{:S(2)}) %copy-start.7) | copy-done | bytes 73752
  9.6 0.0 copy-start.8
  9.6 0.8 copy-done.8
  10.4 76.9 %shard_map.113 = (bf16[24,3072]{1,0:T(8,128)(2,1)S(1)}, bf16[24,3072]{1,0:T(8,128)(2,1)S(1)}) custom-call(s32[1]{0:T(128)S(6)} %copy.14.step_ref, bf16[24,3072]{1,0:T(8,128)(2,1)S(1)} %bitcast.13, bf16[24,3072]{1,0:T(8,128)(2,1)S(1)} %bitcast.14, bf16[3,192,1536]{2,1,0:T(8,128)(2,1)S(1)} %copy-done, bf16[3,64,192]{2,1,0:T(8,128)(2,1)S(1)} %bitcast.15, ...), custom_call_target="tpu_custom_call" | custom-call | flops 1811939328 | bytes 2359296 | tf_op jit(solution)/shard_map/pallas_call | solution.py:384
  87.2 0.7 copy.15
  87.9 0.7 copy.16
Async XLA Ops:
  1.3 1.5 %copy-start = (bf16[3,192,1536]{2,1,0:T(8,128)(2,1)S(1)}, bf16[3,192,1536]{2,1,0:T(8,128)(2,1)}, u32[]{:S(2)}) copy-start(bf16[3,192,1536]{2,1,0:T(8,128)(2,1)} %base_qkv_ref.1) | copy-start | bytes 5308420
  2.8 1.1 %copy-start.1 = (bf16[3,64,1536]{2,1,0:T(8,128)(2,1)S(1)}, bf16[3,64,1536]{2,1,0:T(8,128)(2,1)}, u32[]{:S(2)}) copy-start(bf16[3,64,1536]{2,1,0:T(8,128)(2,1)} %up_qkv_ref.1) | copy-start | bytes 1769476
  3.8 1.1 %copy-start.2 = (bf16[1536,192]{0,1:T(8,128)(2,1)S(1)}, bf16[1536,192]{0,1:T(8,128)(2,1)}, u32[]{:S(2)}) copy-start(bf16[1536,192]{0,1:T(8,128)(2,1)} %param.15) | copy-start | bytes 1769476
  4.9 1.1 %copy-start.3 = (f32[16,3,3072]{2,0,1:T(8,128)S(1)}, f32[16,3,3072]{2,0,1:T(8,128)}, u32[]{:S(2)}) copy-start(f32[16,3,3072]{2,0,1:T(8,128)} %param.18) | copy-start | bytes 1769476
  6.0 0.9 %copy-start.4 = (bf16[1536,64]{0,1:T(8,128)(2,1)S(1)}, bf16[1536,64]{0,1:T(8,128)(2,1)}, u32[]{:S(2)}) copy-start(bf16[1536,64]{0,1:T(8,128)(2,1)} %param.16) | copy-start | bytes 589828
  6.9 0.9 %copy-start.5 = (bf16[1,24,3072]{2,1,0:T(8,128)(2,1)S(1)}, bf16[1,24,3072]{2,1,0:T(8,128)(2,1)}, u32[]{:S(2)}) copy-start(bf16[1,24,3072]{2,1,0:T(8,128)(2,1)} %param.10) | copy-start | bytes 442372
  7.8 0.9 %copy-start.6 = (bf16[1,24,3072]{2,1,0:T(8,128)(2,1)S(1)}, bf16[1,24,3072]{2,1,0:T(8,128)(2,1)}, u32[]{:S(2)}) copy-start(bf16[1,24,3072]{2,1,0:T(8,128)(2,1)} %param.11) | copy-start | bytes 442372
  8.7 0.9 %copy-start.7 = (bf16[3,192,64]{1,2,0:T(8,128)(2,1)S(1)}, bf16[3,192,64]{1,2,0:T(8,128)(2,1)}, u32[]{:S(2)}) copy-start(bf16[3,192,64]{1,2,0:T(8,128)(2,1)} %param.13) | copy-start | bytes 221188
  9.6 0.8 copy-start.8

commit v3 on v2

--- a/solution.py
+++ b/solution.py
@@ -28,6 +28,17 @@
 def plane_kernel(
     n_z,
     step_ref,
+    latents_hbm,
+    noise_hbm,
+    base_qkv_hbm,
+    down_qkv_hbm,
+    up_qkv_hbm,
+    base_out_hbm,
+    down_out_hbm,
+    up_out_hbm,
+    mod_hbm,
+    velocity_ref,
+    next_ref,
     latents_ref,
     noise_ref,
     base_qkv_ref,
@@ -37,8 +48,7 @@
     down_out_ref,
     up_out_ref,
     mod_ref,
-    velocity_ref,
-    next_ref,
+    in_sem,
     latf,
     normed,
     acts,
@@ -67,6 +77,22 @@
     os_sem,
     v_sem,
 ):
+    loads = {}
+    for k, (source, target) in enumerate(
+        (
+            (latents_hbm, latents_ref),
+            (base_qkv_hbm, base_qkv_ref),
+            (down_qkv_hbm, down_qkv_ref),
+            (up_qkv_hbm, up_qkv_ref),
+            (mod_hbm, mod_ref),
+            (base_out_hbm, base_out_ref),
+            (down_out_hbm, down_out_ref),
+            (up_out_hbm, up_out_ref),
+            (noise_hbm, noise_ref),
+        )
+    ):
+        loads[k] = pltpu.make_async_copy(source, target, in_sem.at[k])
+        loads[k].start()
     f, c = lax.axis_index("fsdp"), lax.axis_index("sp")
     z, j = f // PLANE, f % PLANE
     rows, d_model = latents_ref.shape
@@ -111,6 +137,7 @@
     for partner in partners:
         pl.semaphore_signal(barrier, inc=1, device_id=partner, device_id_type=MESH)
 
+    loads[0].wait()
     latf[c] = latents_ref[...].astype(f32)
 
     def merge(h):
@@ -138,10 +165,13 @@
                 w_send.at[h, (j + d) % PLANE], w_recv.at[h, j], w_sem, (h, d - 1), in_plane(d)
             )
 
+    for k in (1, 2, 3):
+        loads[k].wait()
     merge(0)
     send_weights(0)
 
     step_index = step_ref[0]
+    loads[4].wait()
 
     def mod_row(k):
         return mod_ref[k, pl.ds(step_index, 1), :]
@@ -176,10 +206,10 @@
         for d in range(1, PLANE)
     ]
     xs = [send(acts.at[c, :, j], acts.at[c, :, j], xs_sem, (0,), sibling)]
-    for h in range(1, n_head):
-        if h > 1:
-            merge(h)
-        send_weights(h)
+    for h in range(2, n_head):
+        merge(h)
+    for k in (5, 6, 7):
+        loads[k].wait()
     merged_out = (
         base_out_ref[...].astype(f32)
         + lax.dot_general(
@@ -197,6 +227,8 @@
         x3[d - 1].wait_recv()
         came = (j + PLANE - d) % PLANE
         xs.append(send(acts.at[c, :, came], acts.at[c, :, came], xs_sem, (d,), sibling))
+    if n_head > 1:
+        send_weights(1)
     for copy in xs:
         copy.wait_recv()
 
@@ -208,9 +240,13 @@
         return send(view, view, wo_sem, where, device)
 
     pair_copies, far_copies = {}, {}
-    for h in range(n_head):
+    def partial_sums(h):
         for d in range(1, PLANE):
             w_copies[h, d].wait_recv()
+        if h == n_head - 1:
+            for k in range(2):
+                wo_x.append(send_out_rows(j, k, (0, k), x_device))
+                wo_y.append(send_out_rows(j, 1 - k, (1, 1 - k), y_device))
         weights = w_recv[h].reshape(PLANE * w_rows, width)
         for parity, hi in ((1, 1), (1, 0), (0, 1), (0, 0)):
             z_at = 2 * ((z_hi + hi) % 2) + (z_lo + parity) % 2
@@ -230,10 +266,6 @@
                 )
             else:
                 part_own[h, hi] = part
-        if h == min(1, n_head - 1):
-            for k in range(2):
-                wo_x.append(send_out_rows(j, k, (0, k), x_device))
-                wo_y.append(send_out_rows(j, 1 - k, (1, 1 - k), y_device))
 
     def send_far(h):
         pair_copies[h, 1].wait_recv()
@@ -287,18 +319,23 @@
             )
         att_all[z, :, lanes(h, j)] = att_send[h, j]
 
-    send_far(0)
     for h in range(n_head):
-        if h + 1 < n_head:
-            send_far(h + 1)
-        else:
-            wo_x[0].wait_recv()
-            wo_far.append(send_out_rows(x_near, 0, (2, 0), y_device))
-            wo_y[0].wait_recv()
-            wo_far.append(send_out_rows(y_near, 1, (2, 1), x_device))
-        attend(h)
+        partial_sums(h)
+        if h + 2 < n_head:
+            send_weights(h + 2)
+        if h:
+            send_far(h - 1)
+        if h > 1:
+            attend(h - 2)
+    send_far(n_head - 1)
+    for h in range(max(n_head - 2, 0), n_head):
         if h:
             spread(h - 1)
+        attend(h)
+    wo_x[0].wait_recv()
+    wo_far.append(send_out_rows(x_near, 0, (2, 0), y_device))
+    wo_y[0].wait_recv()
+    wo_far.append(send_out_rows(y_near, 1, (2, 1), x_device))
     spread(n_head - 1)
 
     for copy in (wo_x[1], wo_y[1], *wo_far):
@@ -336,6 +373,7 @@
             vel_recv[z] = block_sum
 
     gate = mod_row(2)
+    loads[8].wait()
     position = jnp.full((1, block), step_index.astype(f32), f32)
     step_size = plan_sigma(position + 1.0) - plan_sigma(position)
     noise_size = NOISE_LEVEL * jnp.sqrt(-step_size)
@@ -378,15 +416,28 @@
     f32, bf16 = jnp.float32, jnp.bfloat16
     if half % HEAD_DIM or w_rows % 32 or block != PLANE * w_rows or base_out.shape[1] != w_rows:
         return gather_weights(*args)
+    operands = (
+        base_qkv,
+        down_qkv.swapaxes(1, 2),
+        up_qkv,
+        base_out.T,
+        down_out.T,
+        up_out,
+        modulation.swapaxes(0, 1),
+    )
     padded = -(-rows // 16) * 16
     dma = pltpu.SemaphoreType.DMA
     vmem = pl.BlockSpec(memory_space=pltpu.VMEM)
     velocity, next_rows = pl.pallas_call(
         functools.partial(plane_kernel, n_z),
         out_shape=[jax.ShapeDtypeStruct((rows, d_model), bf16)] * 2,
-        in_specs=[pl.BlockSpec(memory_space=pltpu.SMEM)] + [vmem] * 9,
+        in_specs=[pl.BlockSpec(memory_space=pltpu.SMEM)] + [pl.BlockSpec(memory_space=pl.ANY)] * 9,
         out_specs=[vmem] * 2,
         scratch_shapes=[
+            pltpu.VMEM(latents.shape[1:], bf16),
+            pltpu.VMEM(step_noise.shape[1:], bf16),
+            *[pltpu.VMEM(array.shape, array.dtype) for array in operands],
+            dma((9,)),
             pltpu.VMEM((2, rows, d_model), f32),
             pltpu.VMEM((tokens, d_model), bf16),
             pltpu.VMEM((2, n_z, PLANE, tokens, half), bf16),
@@ -416,7 +467,7 @@
             dma((2, n_z - 1)),
         ],
         compiler_params=pltpu.CompilerParams(
-            collective_id=0, has_side_effects=True, vmem_limit_bytes=48 * 1024 * 1024
+            collective_id=0, has_side_effects=True, vmem_limit_bytes=56 * 1024 * 1024
         ),
         cost_estimate=pl.CostEstimate(
             flops=2 * n_fsdp * tokens * w_rows * 4 * cols,
@@ -427,13 +478,7 @@
         step,
         latents[0],
         step_noise[0],
-        base_qkv,
-        down_qkv.swapaxes(1, 2),
-        up_qkv,
-        base_out.T,
-        down_out.T,
-        up_out,
-        modulation.swapaxes(0, 1),
+        *operands,
     )
     return (velocity[None], next_rows[None])
 

time: 89 us -> 82.1 us (0.922)
  local copies, waits for them, and re-layouts: 10.4 us -> 3.16 us
    unnamed x20 -> x2, local copies, waits for them, and re-layouts: 10.4 us -> 3.16 us
where the time goes in v3:
time: 82.1 us; the launch traced here: 81.2 us
  Pallas kernels  76.7 us (93%)
  local copies, waits for them, and re-layouts  3.16 us (4%)
  between operations  1.29 us (2%)
    pallas_call x1, Pallas kernels, per_device(): pl.pallas_call(functools.partial(plane_kernel, n_z), out_shape=[jax.Shape...  76.7 us
    unnamed x2, local copies, waits for them, and re-layouts  3.16 us

profile of v3, /device:TPU:0, one launch (start us, length us, event | category | flops | bytes accessed | tf_op | source)
XLA Modules:
  0.0 81.2 jit_solution(12666747806716393292)
XLA Ops:
  1.3 76.7 %shard_map.113 = (bf16[24,3072]{1,0:T(8,128)(2,1)}, bf16[24,3072]{1,0:T(8,128)(2,1)}) custom-call(s32[1]{0:T(128)S(6)} %copy.14.step_ref, bf16[24,3072]{1,0:T(8,128)(2,1)} %bitcast.13, bf16[24,3072]{1,0:T(8,128)(2,1)} %bitcast.14, bf16[3,192,1536]{2,1,0:T(8,128)(2,1)} %base_qkv_hbm.1, bf16[3,64,192]{2,1,0:T(8,128)(2,1)} %bitcast.15, ...), custom_call_target="tpu_custom_call" | custom-call | flops 1811939328 | bytes 2359296 | tf_op jit(solution)/shard_map/pallas_call | solution.py:431
  78.0 1.6 %copy.15 = bf16[1,24,3072]{2,1,0:T(8,128)(2,1)} copy(bf16[1,24,3072]{2,1,0:T(8,128)(2,1)} %bitcast.9) | data formatting | bytes 294912
  79.6 1.6 %copy.16 = bf16[1,24,3072]{2,1,0:T(8,128)(2,1)} copy(bf16[1,24,3072]{2,1,0:T(8,128)(2,1)} %bitcast.8) | data formatting | bytes 294912

commit v4 on v3

--- a/solution.py
+++ b/solution.py
@@ -29,7 +29,6 @@
     n_z,
     step_ref,
     latents_hbm,
-    noise_hbm,
     base_qkv_hbm,
     down_qkv_hbm,
     up_qkv_hbm,
@@ -37,12 +36,9 @@
     down_out_hbm,
     up_out_hbm,
     mod_hbm,
-    velocity_ref,
-    next_ref,
+    result_ref,
+    factors_ref,
     latents_ref,
-    noise_ref,
-    base_qkv_ref,
-    down_qkv_ref,
     up_qkv_ref,
     base_out_ref,
     down_out_ref,
@@ -52,8 +48,10 @@
     latf,
     normed,
     acts,
-    w_send,
-    w_recv,
+    base_all,
+    down_all,
+    lowrank,
+    w_all,
     part_send,
     part_recv,
     part_own,
@@ -69,6 +67,7 @@
     x3_sem,
     xs_sem,
     w_sem,
+    down_sem,
     pair_sem,
     far_sem,
     wo_sem,
@@ -77,30 +76,16 @@
     os_sem,
     v_sem,
 ):
-    loads = {}
-    for k, (source, target) in enumerate(
-        (
-            (latents_hbm, latents_ref),
-            (base_qkv_hbm, base_qkv_ref),
-            (down_qkv_hbm, down_qkv_ref),
-            (up_qkv_hbm, up_qkv_ref),
-            (mod_hbm, mod_ref),
-            (base_out_hbm, base_out_ref),
-            (down_out_hbm, down_out_ref),
-            (up_out_hbm, up_out_ref),
-            (noise_hbm, noise_ref),
-        )
-    ):
-        loads[k] = pltpu.make_async_copy(source, target, in_sem.at[k])
-        loads[k].start()
     f, c = lax.axis_index("fsdp"), lax.axis_index("sp")
     z, j = f // PLANE, f % PLANE
     rows, d_model = latents_ref.shape
     tokens = 2 * rows
-    n_head = w_send.shape[0]
+    n_head = w_all.shape[0]
+    own = n_head * HEAD_DIM
+    own_cols = pl.ds(pl.multiple_of(j * own, HEAD_DIM), own)
     block = d_model // n_z
     half = block // 2
-    w_rows = base_qkv_ref.shape[1]
+    w_rows = base_qkv_hbm.shape[1]
     x_at, y_at = j % 2, j // 2
     z_lo, z_hi = z % 2, z // 2
     x_near, y_near = 2 * y_at + 1 - x_at, 2 * (1 - y_at) + x_at
@@ -130,6 +115,21 @@
         copy.start()
         return copy
 
+    loads = {}
+    for k, (source, target) in enumerate(
+        (
+            (latents_hbm, latents_ref),
+            (base_qkv_hbm.at[:, :, own_cols], base_all.at[:, j]),
+            (down_qkv_hbm, down_all.at[j]),
+            (up_qkv_hbm.at[:, :, own_cols], up_qkv_ref),
+            (mod_hbm, mod_ref),
+            (base_out_hbm, base_out_ref),
+            (down_out_hbm, down_out_ref),
+            (up_out_hbm, up_out_ref),
+        )
+    ):
+        loads[k] = pltpu.make_async_copy(source, target, in_sem.at[k])
+        loads[k].start()
     barrier = pltpu.get_barrier_semaphore()
     partners = [sibling]
     partners += [in_plane(d) for d in range(1, PLANE)]
@@ -140,35 +140,30 @@
     loads[0].wait()
     latf[c] = latents_ref[...].astype(f32)
 
-    def merge(h):
-        for g in range(PLANE):
-            at = (g * n_head + h) * HEAD_DIM
-            for p in range(3):
-                lowrank = lax.dot_general(
-                    down_qkv_ref[p],
-                    up_qkv_ref[p, :, at : at + HEAD_DIM],
-                    (((0,), (0,)), ((), ())),
-                    preferred_element_type=f32,
-                )
-                w_send[h, g, :, p * HEAD_DIM : (p + 1) * HEAD_DIM] = (
-                    base_qkv_ref[p, :, at : at + HEAD_DIM].astype(f32) + lowrank
-                ).astype(bf16)
-        w_recv[h, j] = w_send[h, j]
-
     pl.semaphore_wait(barrier, len(partners))
     lat_copy = send(latf.at[c], latf.at[c], lat_sem, (), sibling)
     w_copies = {}
 
     def send_weights(h):
+        lanes_h = slice(h * HEAD_DIM, (h + 1) * HEAD_DIM)
         for d in range(1, PLANE):
-            w_copies[h, d] = send(
-                w_send.at[h, (j + d) % PLANE], w_recv.at[h, j], w_sem, (h, d - 1), in_plane(d)
-            )
-
-    for k in (1, 2, 3):
-        loads[k].wait()
-    merge(0)
+            at = ((j + d) % PLANE) * own + h * HEAD_DIM
+            cols = pl.ds(pl.multiple_of(at, HEAD_DIM), HEAD_DIM)
+            for p in range(3):
+                w_copies[h, d, p] = send(
+                    base_qkv_hbm.at[p, :, cols],
+                    base_all.at[p, j, :, lanes_h],
+                    w_sem,
+                    (h, d - 1, p),
+                    in_plane(d),
+                )
+
     send_weights(0)
+    loads[2].wait()
+    down_copies = [
+        send(down_all.at[j], down_all.at[j], down_sem, (d - 1,), in_plane(d))
+        for d in range(1, PLANE)
+    ]
 
     step_index = step_ref[0]
     loads[4].wait()
@@ -197,8 +192,6 @@
         for d in range(1, n_z)
     ]
     acts[c, z, j] = normed[:, features(z)]
-    if n_head > 1:
-        merge(1)
     for copy in x1:
         copy.wait_recv()
     x3 = [
@@ -206,8 +199,29 @@
         for d in range(1, PLANE)
     ]
     xs = [send(acts.at[c, :, j], acts.at[c, :, j], xs_sem, (0,), sibling)]
-    for h in range(2, n_head):
-        merge(h)
+    for copy in down_copies:
+        copy.wait_recv()
+    for k in (1, 3):
+        loads[k].wait()
+    for p in range(3):
+        for g in range(PLANE):
+            lowrank[p, g] = lax.dot_general(
+                down_all[g, p],
+                up_qkv_ref[p],
+                (((0,), (0,)), ((), ())),
+                preferred_element_type=f32,
+            )
+    position = jnp.full((1, d_model), step_index.astype(f32), f32)
+    step_size = plan_sigma(position + 1.0) - plan_sigma(position)
+    factors_ref[...] = jnp.concatenate(
+        [
+            1.0 + mod_row(2),
+            step_size,
+            NOISE_LEVEL * jnp.sqrt(-step_size),
+            jnp.zeros((factors_ref.shape[0] - 3, d_model), f32),
+        ],
+        axis=0,
+    )
     for k in (5, 6, 7):
         loads[k].wait()
     merged_out = (
@@ -242,12 +256,19 @@
     pair_copies, far_copies = {}, {}
     def partial_sums(h):
         for d in range(1, PLANE):
-            w_copies[h, d].wait_recv()
+            for p in range(3):
+                w_copies[h, d, p].wait_recv()
         if h == n_head - 1:
             for k in range(2):
                 wo_x.append(send_out_rows(j, k, (0, k), x_device))
                 wo_y.append(send_out_rows(j, 1 - k, (1, 1 - k), y_device))
-        weights = w_recv[h].reshape(PLANE * w_rows, width)
+        lanes_h = slice(h * HEAD_DIM, (h + 1) * HEAD_DIM)
+        for p in range(3):
+            merged = (base_all[p, :, :, lanes_h].astype(f32) + lowrank[p, :, :, lanes_h]).astype(bf16)
+            w_all[h, :, p * HEAD_DIM : (p + 1) * HEAD_DIM] = merged.reshape(
+                PLANE * w_rows, HEAD_DIM
+            )
+        weights = w_all[h]
         for parity, hi in ((1, 1), (1, 0), (0, 1), (0, 0)):
             z_at = 2 * ((z_hi + hi) % 2) + (z_lo + parity) % 2
             part = jnp.dot(
@@ -372,25 +393,12 @@
         else:
             vel_recv[z] = block_sum
 
-    gate = mod_row(2)
-    loads[8].wait()
-    position = jnp.full((1, block), step_index.astype(f32), f32)
-    step_size = plan_sigma(position + 1.0) - plan_sigma(position)
-    noise_size = NOISE_LEVEL * jnp.sqrt(-step_size)
     for copy in v_copies:
         copy.wait_recv()
     for s in range(n_z):
-        cols = slice(s * block, (s + 1) * block)
-        block_out = vel_recv[s].astype(f32)[:rows]
-        velocity = ((1.0 + gate[:, cols]) * block_out).astype(bf16)
-        velocity_ref[:, cols] = velocity
-        next_ref[:, cols] = (
-            latf[c, :, cols]
-            + step_size * velocity.astype(f32)
-            + noise_size * noise_ref[:, cols].astype(f32)
-        ).astype(bf16)
-
-    every = [lat_copy, os_copy, *x1, *x3, *xs, *wo_x, *wo_y, *wo_far, *v_copies]
+        result_ref[:, s * block : (s + 1) * block] = vel_recv[s, :rows]
+
+    every = [lat_copy, os_copy, *x1, *x3, *xs, *wo_x, *wo_y, *wo_far, *v_copies, *down_copies]
     for group in (w_copies, pair_copies, far_copies, at_copies, ag_copies):
         every += list(group.values())
     for copy in every:
@@ -428,21 +436,26 @@
     padded = -(-rows // 16) * 16
     dma = pltpu.SemaphoreType.DMA
     vmem = pl.BlockSpec(memory_space=pltpu.VMEM)
-    velocity, next_rows = pl.pallas_call(
+    block_out, factors = pl.pallas_call(
         functools.partial(plane_kernel, n_z),
-        out_shape=[jax.ShapeDtypeStruct((rows, d_model), bf16)] * 2,
-        in_specs=[pl.BlockSpec(memory_space=pltpu.SMEM)] + [pl.BlockSpec(memory_space=pl.ANY)] * 9,
+        out_shape=[
+            jax.ShapeDtypeStruct((rows, d_model), bf16),
+            jax.ShapeDtypeStruct((8, d_model), f32),
+        ],
+        in_specs=[pl.BlockSpec(memory_space=pltpu.SMEM)] + [pl.BlockSpec(memory_space=pl.ANY)] * 8,
         out_specs=[vmem] * 2,
         scratch_shapes=[
             pltpu.VMEM(latents.shape[1:], bf16),
-            pltpu.VMEM(step_noise.shape[1:], bf16),
-            *[pltpu.VMEM(array.shape, array.dtype) for array in operands],
-            dma((9,)),
+            pltpu.VMEM((*up_qkv.shape[:2], cols // PLANE), bf16),
+            *[pltpu.VMEM(array.shape, array.dtype) for array in operands[3:]],
+            dma((8,)),
             pltpu.VMEM((2, rows, d_model), f32),
             pltpu.VMEM((tokens, d_model), bf16),
             pltpu.VMEM((2, n_z, PLANE, tokens, half), bf16),
-            pltpu.VMEM((n_head, PLANE, w_rows, width), bf16),
-            pltpu.VMEM((n_head, PLANE, w_rows, width), bf16),
+            pltpu.VMEM((3, PLANE, w_rows, cols // PLANE), bf16),
+            pltpu.VMEM((PLANE, *operands[1].shape), bf16),
+            pltpu.VMEM((3, PLANE, w_rows, cols // PLANE), f32),
+            pltpu.VMEM((n_head, PLANE * w_rows, width), bf16),
             pltpu.VMEM((n_head, 3, PLANE * tokens, width), bf16),
             pltpu.VMEM((n_head, 3, PLANE * tokens, width), bf16),
             pltpu.VMEM((n_head, 2, PLANE * tokens, width), f32),
@@ -457,7 +470,8 @@
             dma((2, n_z - 1)),
             dma((2, PLANE - 1)),
             dma((2, PLANE)),
-            dma((2, n_head, PLANE - 1)),
+            dma((2, n_head, PLANE - 1, 3)),
+            dma((2, PLANE - 1)),
             dma((2, n_head, 2)),
             dma((2, n_head)),
             dma((2, 3, 2)),
@@ -477,10 +491,15 @@
     )(
         step,
         latents[0],
-        step_noise[0],
         *operands,
     )
-    return (velocity[None], next_rows[None])
+    velocity = (factors[0:1] * block_out.astype(f32)).astype(bf16)
+    next_rows = (
+        latents[0].astype(f32)
+        + factors[1:2] * velocity.astype(f32)
+        + factors[2:3] * step_noise[0].astype(f32)
+    )
+    return (velocity[None], next_rows.astype(bf16)[None])
 
 
 def gather_weights(

time: 82.1 us -> 85.9 us (1.046)
  Pallas kernels: 76.7 us -> 80.5 us
  local copies, waits for them, and re-layouts: 3.16 us -> 1.08 us
  other arithmetic: 0 us -> 1.72 us
    pallas_call x1, Pallas kernels: 76.7 us -> 80.5 us  [per_device(): pl.pallas_call(functools.partial(plane_kernel, n_z), out_shape=[jax.Shape...]
    unnamed x2 -> x4, local copies, waits for them, and re-layouts: 3.16 us -> 0.01 us
    broadcast_in_dim x0 -> x1, other arithmetic: none -> 1.72 us  [per_device(): return (velocity[None], next_rows.astype(bf16)[None])]
    slice x0 -> x1, local copies, waits for them, and re-layouts: none -> 1.07 us  [per_device(): factors[1:2] * velocity.astype(f32)]
where the time goes in v4:
time: 85.9 us; the launch traced here: 84.7 us
  Pallas kernels  80.5 us (94%)
  other arithmetic  1.72 us (2%)
  between operations  1.32 us (2%)
  local copies, waits for them, and re-layouts  1.08 us (1%)
    pallas_call x1, Pallas kernels, per_device(): pl.pallas_call(functools.partial(plane_kernel, n_z), out_shape=[jax.Shape...  80.5 us

profile of v4, /device:TPU:0, one launch (start us, length us, event | category | flops | bytes accessed | tf_op | source)
XLA Modules:
  0.0 84.7 jit_solution(5243261653331744372)
XLA Ops:
  1.3 0.0 copy-start
  1.3 0.0 copy-start.1
  1.3 80.5 %shard_map.113 = (bf16[24,3072]{1,0:T(8,128)(2,1)}, f32[8,3072]{1,0:T(8,128)}) custom-call(s32[1]{0:T(128)S(6)} %copy.12.step_ref, bf16[24,3072]{1,0:T(8,128)(2,1)} %bitcast.16, bf16[3,192,1536]{2,1,0:T(8,128)(2,1)} %base_qkv_hbm.1, bf16[3,64,192]{2,1,0:T(8,128)(2,1)} %bitcast.23, bf16[3,64,1536]{2,1,0:T(8,128)(2,1)} %up_qkv_hbm.1, ...), custom_call_target="tpu_custom_call" | custom-call | flops 1811939328 | bytes 2359296 | tf_op jit(solution)/shard_map/pallas_call | solution.py:439
  81.9 1.1 %fusion.4 = (f32[1,3072]{1,0:T(1,128)S(1)}, f32[1,3072]{1,0:T(1,128)S(1)}, f32[1,3072]{1,0:T(1,128)S(1)}) fusion(f32[8,3072]{1,0:T(8,128)} %get-tuple-element.4), kind=kLoop, calls=%fused_computation.6 | loop fusion | bytes 73728 | tf_op jit(solution)/shard_map/slice | solution.py:499
  82.9 0.0 copy-done
  82.9 0.0 copy-done.1
  83.0 1.7 %fusion.2 = (bf16[1,24,3072]{2,1,0:T(8,128)(2,1)}, bf16[1,24,3072]{2,1,0:T(8,128)(2,1)}) fusion(bf16[1,24,3072]{2,1,0:T(8,128)(2,1)S(1)} %copy-done, f32[3072]{0:T(1024)S(1)} %bitcast.18, f32[3072]{0:T(1024)S(1)} %bitcast.17, bf16[24,3072]{1,0:T(8,128)(2,1)} %get-tuple-element.5, f32[3072]{0:T(1024)S(1)} %bitcast.19, bf16[1,24,3072]{2,1,0:T(8,128)(2,1)S(1)} %copy-done.1), kind=kLoop, calls=%fused_computation.4 | loop fusion | flops 811008 | bytes 774144 | tf_op jit(solution)/shard_map/broadcast_in_dim | solution.py:502
Async XLA Ops:
  1.3 81.7 %copy-start = (bf16[1,24,3072]{2,1,0:T(8,128)(2,1)S(1)}, bf16[1,24,3072]{2,1,0:T(8,128)(2,1)}, u32[]{:S(2)}) copy-start(bf16[1,24,3072]{2,1,0:T(8,128)(2,1)} %param.11) | copy-start | bytes 442372
  1.3 81.7 %copy-start.1 = (bf16[1,24,3072]{2,1,0:T(8,128)(2,1)S(1)}, bf16[1,24,3072]{2,1,0:T(8,128)(2,1)}, u32[]{:S(2)}) copy-start(bf16[1,24,3072]{2,1,0:T(8,128)(2,1)} %param.10) | copy-start | bytes 442372

commit v5 on v3

--- a/solution.py
+++ b/solution.py
@@ -29,7 +29,6 @@
     n_z,
     step_ref,
     latents_hbm,
-    noise_hbm,
     base_qkv_hbm,
     down_qkv_hbm,
     up_qkv_hbm,
@@ -37,10 +36,11 @@
     down_out_hbm,
     up_out_hbm,
     mod_hbm,
-    velocity_ref,
-    next_ref,
+    result_ref,
+    gate_ref,
+    step_size_ref,
+    noise_size_ref,
     latents_ref,
-    noise_ref,
     base_qkv_ref,
     down_qkv_ref,
     up_qkv_ref,
@@ -88,7 +88,6 @@
             (base_out_hbm, base_out_ref),
             (down_out_hbm, down_out_ref),
             (up_out_hbm, up_out_ref),
-            (noise_hbm, noise_ref),
         )
     ):
         loads[k] = pltpu.make_async_copy(source, target, in_sem.at[k])
@@ -141,17 +140,18 @@
     latf[c] = latents_ref[...].astype(f32)
 
     def merge(h):
-        for g in range(PLANE):
-            at = (g * n_head + h) * HEAD_DIM
-            for p in range(3):
-                lowrank = lax.dot_general(
-                    down_qkv_ref[p],
-                    up_qkv_ref[p, :, at : at + HEAD_DIM],
-                    (((0,), (0,)), ((), ())),
-                    preferred_element_type=f32,
-                )
+        for p in range(3):
+            ats = [(g * n_head + h) * HEAD_DIM for g in range(PLANE)]
+            lowrank = lax.dot_general(
+                down_qkv_ref[p],
+                jnp.concatenate([up_qkv_ref[p, :, at : at + HEAD_DIM] for at in ats], axis=1),
+                (((0,), (0,)), ((), ())),
+                preferred_element_type=f32,
+            )
+            for g, at in enumerate(ats):
                 w_send[h, g, :, p * HEAD_DIM : (p + 1) * HEAD_DIM] = (
-                    base_qkv_ref[p, :, at : at + HEAD_DIM].astype(f32) + lowrank
+                    base_qkv_ref[p, :, at : at + HEAD_DIM].astype(f32)
+                    + lowrank[:, g * HEAD_DIM : (g + 1) * HEAD_DIM]
                 ).astype(bf16)
         w_recv[h, j] = w_send[h, j]
 
@@ -186,28 +186,34 @@
     def features(z_at):
         return pl.ds(pl.multiple_of(z_at * block + c * half, half), half)
 
+    own_half = pl.ds(pl.multiple_of(c * half, HEAD_DIM), half)
     x1 = [
         send(
             normed.at[:, features((z + d) % n_z)],
-            acts.at[c, z, j],
+            acts.at[z, j, :, own_half],
             x1_sem,
             (d - 1,),
             in_column(d),
         )
         for d in range(1, n_z)
     ]
-    acts[c, z, j] = normed[:, features(z)]
+    acts[z, j, :, own_half] = normed[:, features(z)]
     if n_head > 1:
         merge(1)
     for copy in x1:
         copy.wait_recv()
     x3 = [
-        send(acts.at[c, :, j], acts.at[c, :, j], x3_sem, (d - 1,), in_plane(d))
+        send(acts.at[:, j, :, own_half], acts.at[:, j, :, own_half], x3_sem, (d - 1,), in_plane(d))
         for d in range(1, PLANE)
     ]
-    xs = [send(acts.at[c, :, j], acts.at[c, :, j], xs_sem, (0,), sibling)]
+    xs = [send(acts.at[:, j, :, own_half], acts.at[:, j, :, own_half], xs_sem, (0,), sibling)]
     for h in range(2, n_head):
         merge(h)
+    gate_ref[...] = 1.0 + mod_row(2)
+    position = jnp.full((1, d_model), step_index.astype(f32), f32)
+    step_size = plan_sigma(position + 1.0) - plan_sigma(position)
+    step_size_ref[...] = step_size
+    noise_size_ref[...] = NOISE_LEVEL * jnp.sqrt(-step_size)
     for k in (5, 6, 7):
         loads[k].wait()
     merged_out = (
@@ -226,7 +232,7 @@
     for d in range(1, PLANE):
         x3[d - 1].wait_recv()
         came = (j + PLANE - d) % PLANE
-        xs.append(send(acts.at[c, :, came], acts.at[c, :, came], xs_sem, (d,), sibling))
+        xs.append(send(acts.at[:, came, :, own_half], acts.at[:, came, :, own_half], xs_sem, (d,), sibling))
     if n_head > 1:
         send_weights(1)
     for copy in xs:
@@ -248,24 +254,28 @@
                 wo_x.append(send_out_rows(j, k, (0, k), x_device))
                 wo_y.append(send_out_rows(j, 1 - k, (1, 1 - k), y_device))
         weights = w_recv[h].reshape(PLANE * w_rows, width)
-        for parity, hi in ((1, 1), (1, 0), (0, 1), (0, 0)):
-            z_at = 2 * ((z_hi + hi) % 2) + (z_lo + parity) % 2
+        for parity in (1, 0):
+            z_row = (z_lo + parity) % 2
             part = jnp.dot(
-                acts[0, z_at].reshape(PLANE * tokens, half),
-                weights[:half],
-                preferred_element_type=f32,
-            ) + jnp.dot(
-                acts[1, z_at].reshape(PLANE * tokens, half),
-                weights[half:],
+                jnp.concatenate(
+                    [
+                        acts[2 * ((z_hi + hi) % 2) + z_row].reshape(PLANE * tokens, block)
+                        for hi in (1, 0)
+                    ],
+                    axis=0,
+                ),
+                weights,
                 preferred_element_type=f32,
             )
-            if parity:
-                part_send[h, hi] = part.astype(bf16)
-                pair_copies[h, hi] = send(
-                    part_send.at[h, hi], part_recv.at[h, hi], pair_sem, (h, hi), z_pair
-                )
-            else:
-                part_own[h, hi] = part
+            for hi in (1, 0):
+                rows_hi = part[(1 - hi) * PLANE * tokens : (2 - hi) * PLANE * tokens]
+                if parity:
+                    part_send[h, hi] = rows_hi.astype(bf16)
+                    pair_copies[h, hi] = send(
+                        part_send.at[h, hi], part_recv.at[h, hi], pair_sem, (h, hi), z_pair
+                    )
+                else:
+                    part_own[h, hi] = rows_hi
 
     def send_far(h):
         pair_copies[h, 1].wait_recv()
@@ -356,12 +366,18 @@
         for k in range(2):
             at = s * tokens + k * rows
             out_half[k, s] = out[at : at + rows]
-    os_copy = send(out_half.at[1 - c], out_sib, os_sem, (), sibling)
-    os_copy.wait_recv()
+    order = list(range(1, n_z)) + [0]
+    os_copies = []
+    for d in order:
+        z_at = (z + d) % n_z
+        os_copies.append(
+            send(out_half.at[1 - c, z_at], out_sib.at[z_at], os_sem, (d,), sibling)
+        )
     pad = jnp.zeros((vel_send.shape[1] - rows, block), f32)
     v_copies = []
-    for d in list(range(1, n_z)) + [0]:
+    for k, d in enumerate(order):
         z_at = (z + d) % n_z
+        os_copies[k].wait_recv()
         block_sum = out_half[c, z_at] + out_sib[z_at]
         block_sum = jnp.concatenate([block_sum, pad], axis=0).astype(bf16)
         if d:
@@ -371,26 +387,12 @@
             )
         else:
             vel_recv[z] = block_sum
-
-    gate = mod_row(2)
-    loads[8].wait()
-    position = jnp.full((1, block), step_index.astype(f32), f32)
-    step_size = plan_sigma(position + 1.0) - plan_sigma(position)
-    noise_size = NOISE_LEVEL * jnp.sqrt(-step_size)
     for copy in v_copies:
         copy.wait_recv()
     for s in range(n_z):
-        cols = slice(s * block, (s + 1) * block)
-        block_out = vel_recv[s].astype(f32)[:rows]
-        velocity = ((1.0 + gate[:, cols]) * block_out).astype(bf16)
-        velocity_ref[:, cols] = velocity
-        next_ref[:, cols] = (
-            latf[c, :, cols]
-            + step_size * velocity.astype(f32)
-            + noise_size * noise_ref[:, cols].astype(f32)
-        ).astype(bf16)
-
-    every = [lat_copy, os_copy, *x1, *x3, *xs, *wo_x, *wo_y, *wo_far, *v_copies]
+        result_ref[:, s * block : (s + 1) * block] = vel_recv[s, :rows]
+
+    every = [lat_copy, *os_copies, *x1, *x3, *xs, *wo_x, *wo_y, *wo_far, *v_copies]
     for group in (w_copies, pair_copies, far_copies, at_copies, ag_copies):
         every += list(group.values())
     for copy in every:
@@ -428,19 +430,19 @@
     padded = -(-rows // 16) * 16
     dma = pltpu.SemaphoreType.DMA
     vmem = pl.BlockSpec(memory_space=pltpu.VMEM)
-    velocity, next_rows = pl.pallas_call(
+    block_out, gate, step_size, noise_size = pl.pallas_call(
         functools.partial(plane_kernel, n_z),
-        out_shape=[jax.ShapeDtypeStruct((rows, d_model), bf16)] * 2,
-        in_specs=[pl.BlockSpec(memory_space=pltpu.SMEM)] + [pl.BlockSpec(memory_space=pl.ANY)] * 9,
-        out_specs=[vmem] * 2,
+        out_shape=[jax.ShapeDtypeStruct((rows, d_model), bf16)]
+        + [jax.ShapeDtypeStruct((1, d_model), f32)] * 3,
+        in_specs=[pl.BlockSpec(memory_space=pltpu.SMEM)] + [pl.BlockSpec(memory_space=pl.ANY)] * 8,
+        out_specs=[vmem] * 4,
         scratch_shapes=[
             pltpu.VMEM(latents.shape[1:], bf16),
-            pltpu.VMEM(step_noise.shape[1:], bf16),
             *[pltpu.VMEM(array.shape, array.dtype) for array in operands],
-            dma((9,)),
+            dma((8,)),
             pltpu.VMEM((2, rows, d_model), f32),
             pltpu.VMEM((tokens, d_model), bf16),
-            pltpu.VMEM((2, n_z, PLANE, tokens, half), bf16),
+            pltpu.VMEM((n_z, PLANE, tokens, block), bf16),
             pltpu.VMEM((n_head, PLANE, w_rows, width), bf16),
             pltpu.VMEM((n_head, PLANE, w_rows, width), bf16),
             pltpu.VMEM((n_head, 3, PLANE * tokens, width), bf16),
@@ -463,7 +465,7 @@
             dma((2, 3, 2)),
             dma((2, n_head, PLANE - 1)),
             dma((2, n_head, n_z - 1)),
-            dma((2,)),
+            dma((2, n_z)),
             dma((2, n_z - 1)),
         ],
         compiler_params=pltpu.CompilerParams(
@@ -477,10 +479,15 @@
     )(
         step,
         latents[0],
-        step_noise[0],
         *operands,
     )
-    return (velocity[None], next_rows[None])
+    velocity = (gate * block_out.astype(f32)).astype(bf16)
+    next_rows = (
+        latents[0].astype(f32)
+        + step_size * velocity.astype(f32)
+        + noise_size * step_noise[0].astype(f32)
+    )
+    return (velocity[None], next_rows.astype(bf16)[None])
 
 
 def gather_weights(

time: 82.1 us -> 80.6 us (0.982)
  local copies, waits for them, and re-layouts: 3.16 us -> 0.01 us
  other arithmetic: 0 us -> 1.75 us
    unnamed x2 -> x4, local copies, waits for them, and re-layouts: 3.16 us -> 0.01 us
    broadcast_in_dim x0 -> x1, other arithmetic: none -> 1.75 us  [per_device(): return (velocity[None], next_rows.astype(bf16)[None])]
where the time goes in v5:
time: 80.6 us; the launch traced here: 79.8 us
  Pallas kernels  76.8 us (95%)
  other arithmetic  1.75 us (2%)
  between operations  1.32 us (2%)
    pallas_call x1, Pallas kernels, per_device(): pl.pallas_call(functools.partial(plane_kernel, n_z), out_shape=[jax.Shape...  76.8 us
    broadcast_in_dim x1, other arithmetic, per_device(): return (velocity[None], next_rows.astype(bf16)[None])  1.75 us

profile of v5, /device:TPU:0, one launch (start us, length us, event | category | flops | bytes accessed | tf_op | source)
XLA Modules:
  0.0 79.8 jit_solution(15575503153171508809)
XLA Ops:
  1.3 0.0 copy-start
  1.3 0.0 copy-start.1
  1.3 76.8 %shard_map.113 = (bf16[24,3072]{1,0:T(8,128)(2,1)}, f32[1,3072]{1,0:T(1,128)}, f32[1,3072]{1,0:T(1,128)}, f32[1,3072]{1,0:T(1,128)}) custom-call(s32[1]{0:T(128)S(6)} %copy.12.step_ref, bf16[24,3072]{1,0:T(8,128)(2,1)} %bitcast.16, bf16[3,192,1536]{2,1,0:T(8,128)(2,1)} %base_qkv_hbm.1, bf16[3,64,192]{2,1,0:T(8,128)(2,1)} %bitcast.23, ...), custom_call_target="tpu_custom_call" | custom-call | flops 1811939328 | bytes 2359296 | tf_op jit(solution)/shard_map/pallas_call | solution.py:433
  78.1 0.0 copy-done
  78.1 0.0 copy-done.1
  78.1 1.7 %fusion.2 = (bf16[1,24,3072]{2,1,0:T(8,128)(2,1)}, bf16[1,24,3072]{2,1,0:T(8,128)(2,1)}) fusion(bf16[1,24,3072]{2,1,0:T(8,128)(2,1)S(1)} %copy-done, f32[3072]{0:T(1024)} %bitcast.19, f32[3072]{0:T(1024)} %bitcast.18, bf16[24,3072]{1,0:T(8,128)(2,1)} %get-tuple-element.7, f32[3072]{0:T(1024)} %bitcast.17, bf16[1,24,3072]{2,1,0:T(8,128)(2,1)S(1)} %copy-done.1), kind=kLoop, calls=%fused_computation.4 | loop fusion | flops 811008 | bytes 774144 | tf_op jit(solution)/shard_map/broadcast_in_dim | solution.py:490
Async XLA Ops:
  1.3 76.8 %copy-start = (bf16[1,24,3072]{2,1,0:T(8,128)(2,1)S(1)}, bf16[1,24,3072]{2,1,0:T(8,128)(2,1)}, u32[]{:S(2)}) copy-start(bf16[1,24,3072]{2,1,0:T(8,128)(2,1)} %param.11) | copy-start | bytes 442372
  1.3 76.8 %copy-start.1 = (bf16[1,24,3072]{2,1,0:T(8,128)(2,1)S(1)}, bf16[1,24,3072]{2,1,0:T(8,128)(2,1)}, u32[]{:S(2)}) copy-start(bf16[1,24,3072]{2,1,0:T(8,128)(2,1)} %param.10) | copy-start | bytes 442372

commit v6 on v5

--- a/solution.py
+++ b/solution.py
@@ -246,6 +246,12 @@
         return send(view, view, wo_sem, where, device)
 
     pair_copies, far_copies = {}, {}
+
+    def send_pair(h, hi):
+        pair_copies[h, hi] = send(
+            part_send.at[h, hi], part_recv.at[h, hi], pair_sem, (h, hi), z_pair
+        )
+
     def partial_sums(h):
         for d in range(1, PLANE):
             w_copies[h, d].wait_recv()
@@ -271,9 +277,8 @@
                 rows_hi = part[(1 - hi) * PLANE * tokens : (2 - hi) * PLANE * tokens]
                 if parity:
                     part_send[h, hi] = rows_hi.astype(bf16)
-                    pair_copies[h, hi] = send(
-                        part_send.at[h, hi], part_recv.at[h, hi], pair_sem, (h, hi), z_pair
-                    )
+                    if hi or h < n_head - 1:
+                        send_pair(h, hi)
                 else:
                     part_own[h, hi] = rows_hi
 
@@ -281,6 +286,8 @@
         pair_copies[h, 1].wait_recv()
         part_send[h, 2] = (part_own[h, 1] + part_recv[h, 1].astype(f32)).astype(bf16)
         far_copies[h] = send(part_send.at[h, 2], part_recv.at[h, 2], far_sem, (h,), z_far)
+        if h == n_head - 1:
+            send_pair(h, 0)
 
     at_copies, ag_copies = {}, {}
 

time: 80.6 us -> 77.5 us (0.962)
  Pallas kernels: 76.8 us -> 73.6 us
    pallas_call x1, Pallas kernels: 76.8 us -> 73.6 us  [per_device(): pl.pallas_call(functools.partial(plane_kernel, n_z), out_shape=[jax.Shape...]
where the time goes in v6:
time: 77.5 us; the launch traced here: 76.7 us
  Pallas kernels  73.6 us (95%)
  other arithmetic  1.75 us (2%)
  between operations  1.32 us (2%)
    pallas_call x1, Pallas kernels, per_device(): pl.pallas_call(functools.partial(plane_kernel, n_z), out_shape=[jax.Shape...  73.6 us
    broadcast_in_dim x1, other arithmetic, per_device(): return (velocity[None], next_rows.astype(bf16)[None])  1.75 us

profile of v6, /device:TPU:0, one launch (start us, length us, event | category | flops | bytes accessed | tf_op | source)
XLA Modules:
  0.0 76.7 jit_solution(17773929960043517690)
XLA Ops:
  1.3 0.0 copy-start
  1.3 0.0 copy-start.1
  1.3 73.6 %shard_map.113 = (bf16[24,3072]{1,0:T(8,128)(2,1)}, f32[1,3072]{1,0:T(1,128)}, f32[1,3072]{1,0:T(1,128)}, f32[1,3072]{1,0:T(1,128)}) custom-call(s32[1]{0:T(128)S(6)} %copy.12.step_ref, bf16[24,3072]{1,0:T(8,128)(2,1)} %bitcast.16, bf16[3,192,1536]{2,1,0:T(8,128)(2,1)} %base_qkv_hbm.1, bf16[3,64,192]{2,1,0:T(8,128)(2,1)} %bitcast.23, ...), custom_call_target="tpu_custom_call" | custom-call | flops 1811939328 | bytes 2359296 | tf_op jit(solution)/shard_map/pallas_call | solution.py:440
  74.9 0.0 copy-done
  74.9 0.0 copy-done.1
  74.9 1.7 %fusion.2 = (bf16[1,24,3072]{2,1,0:T(8,128)(2,1)}, bf16[1,24,3072]{2,1,0:T(8,128)(2,1)}) fusion(bf16[1,24,3072]{2,1,0:T(8,128)(2,1)S(1)} %copy-done, f32[3072]{0:T(1024)} %bitcast.19, f32[3072]{0:T(1024)} %bitcast.18, bf16[24,3072]{1,0:T(8,128)(2,1)} %get-tuple-element.7, f32[3072]{0:T(1024)} %bitcast.17, bf16[1,24,3072]{2,1,0:T(8,128)(2,1)S(1)} %copy-done.1), kind=kLoop, calls=%fused_computation.4 | loop fusion | flops 811008 | bytes 774144 | tf_op jit(solution)/shard_map/broadcast_in_dim | solution.py:497
Async XLA Ops:
  1.3 73.6 %copy-start = (bf16[1,24,3072]{2,1,0:T(8,128)(2,1)S(1)}, bf16[1,24,3072]{2,1,0:T(8,128)(2,1)}, u32[]{:S(2)}) copy-start(bf16[1,24,3072]{2,1,0:T(8,128)(2,1)} %param.11) | copy-start | bytes 442372
  1.3 73.6 %copy-start.1 = (bf16[1,24,3072]{2,1,0:T(8,128)(2,1)S(1)}, bf16[1,24,3072]{2,1,0:T(8,128)(2,1)}, u32[]{:S(2)}) copy-start(bf16[1,24,3072]{2,1,0:T(8,128)(2,1)} %param.10) | copy-start | bytes 442372
